TPU v7x, 512 devices: a whole 4x4x16 slice. The times are simulated.
512 devices in a mesh: shard: 64 (over x, z), tp: 8 (over y, core).
Axes of the slice: x: 4, y: 4, z: 16, core: 2. Of those that a mesh axis runs over, the one named last changes fastest.
Arguments:
- hidden: bfloat16 [32768, 4096], P('shard', 'tp'), may hold values from -48 to 48
- latents: bfloat16 [512, 4096], P(None, 'tp'), may hold values from -4 to 4
- lengths: int32 [64, 4], P('shard'), may hold values from 1 to 256, 512 in all within a row
- probes: int32 [256, 8], P('shard'), may hold values from 0 to 511, as said below
- cluster_slot: int32 [512], replicated, may hold values from 0 to 511, as said below
- slab_sizes: int32 [512], replicated, may hold values from 1 to 128, as said below
- passages: bfloat16 [512, 128, 4096], P('shard', None, 'tp'), may hold values from -6 to 6
Outputs:
- scores: float32 [256, 8, 128], P('shard', None, 'tp')
Inputs may be any that keep to these rules, and one draw needn't show every extreme that they name: `slab_sizes`: some cluster holds exactly 128 passages. `cluster_slot`: a permutation of the slots. A query's probes are distinct clusters; of the 32 probes of one pack, at most 4 name clusters whose slots lie on one index of shard (slots i * 8 to (i + 1) * 8 - 1), and exactly 4 do for some index in every pack.
All inputs are finite; a program needn't handle non-finite values.
Results may differ from a plain program's by a relative error of at most 0.009.
Values may be sent and summed in bfloat16 or wider, within the bound.
No kernel may reach another device: no remote copies, remote signals or barrier semaphores. Data moves between devices by JAX's collectives and lax.ppermute only.
A program may use at most 64 MiB of HBM per device.

v0:
```python
import math

import jax
import jax.numpy as jnp
from jax import lax
from jax.sharding import PartitionSpec as P

D = 4096
HEADS = 8


def per_device(hidden, latents, lengths, probes, cluster_slot, slab_sizes, passages):
    tokens_here = hidden.shape[0]
    width_here = hidden.shape[1]
    head_size = D // HEADS
    heads_here = width_here // head_size
    latent_count = latents.shape[0]
    lat = latents.reshape(latent_count, heads_here, head_size)
    states = hidden.reshape(tokens_here, heads_here, head_size)
    logits = jnp.einsum(
        "thd,lhd->htl", states, lat, preferred_element_type=jnp.float32
    ) / math.sqrt(head_size)
    weights = jax.nn.softmax(logits, axis=-1).astype(jnp.bfloat16)
    attended = jnp.einsum("htl,lhd->thd", weights, lat, preferred_element_type=jnp.float32)
    attended = attended.reshape(tokens_here, width_here).astype(jnp.bfloat16)
    lens = lengths[0]
    ends = jnp.cumsum(lens)
    starts = ends - lens
    position = jnp.arange(tokens_here, dtype=jnp.int32)
    member = ((position[None, :] >= starts[:, None]) & (position[None, :] < ends[:, None])).astype(
        jnp.bfloat16
    )
    pooled = jnp.dot(member, attended, preferred_element_type=jnp.float32) / lens[:, None].astype(
        jnp.float32
    )
    squares = lax.psum(jnp.sum(pooled * pooled, axis=-1), "tp")
    query = (pooled / jnp.sqrt(squares[:, None] + 1e-06)).astype(jnp.bfloat16)
    capacity = passages.shape[1]
    requests = query.shape[0]
    nprobe = probes.shape[1]
    partial_scores = jnp.einsum(
        "qd,scd->qsc",
        lax.all_gather(query, "shard", axis=0, tiled=True),
        passages,
        preferred_element_type=jnp.float32,
    )
    tiles = lax.all_to_all(partial_scores, "shard", split_axis=0, concat_axis=1, tiled=True)
    slots = jnp.take(cluster_slot, probes)
    index = jnp.broadcast_to(slots[:, :, None], (requests, nprobe, capacity))
    mine = jnp.take_along_axis(tiles, index, axis=1)
    summed = lax.psum_scatter(mine, "tp", scatter_dimension=2, tiled=True)
    cap_here = summed.shape[2]
    column = lax.axis_index("tp") * cap_here + jnp.arange(cap_here, dtype=jnp.int32)
    sizes = jnp.take(slab_sizes, probes)
    valid = column[None, None, :] < sizes[:, :, None]
    return jnp.where(valid, summed, jnp.float32(0.0))


def solution(mesh):
    placed = (
        P("shard", "tp"),
        P(None, "tp"),
        P("shard", None),
        P("shard", None),
        P(),
        P(),
        P("shard", None, "tp"),
    )
    return jax.shard_map(
        per_device, mesh=mesh, in_specs=placed, out_specs=P("shard", None, "tp"), check_vma=False
    )
```

profile of v0, /device:TPU:1, one launch (start us, length us, event | category | flops | bytes accessed | tf_op | source)
XLA Modules:
  0.0 232.9 jit_solution(3572695575971267765)
XLA Ops:
  6.5 0.7 bitcast_convert_fusion
  7.3 0.8 reduce-window.7
  8.1 0.7 bitcast_subtract_fusion
  8.8 1.7 fusion.9
  10.5 0.2 fusion.1
  10.7 0.8 copy-done.3
  11.5 0.7 fusion.3
  12.2 18.6 %psum.7 = f32[4]{0:T(128)S(1)} all-reduce(f32[4]{0:T(128)S(1)} %get-tuple-element.10), channel_id=1, replica_groups=mesh['shard'=64,'tp'=8] {'tp'}, use_global_device_ids=true, to_apply=%region_4.6 | all-reduce | flops 4 | bytes 32 | tf_op jit(solution)/shard_map/psum | solution.py:36
  31.0 64.4 %all-gather = bf16[64,4,512]{2,1,0:T(4,128)(2,1)S(1)} all-gather(bf16[1,4,512]{2,1,0:T(4,128)(2,1)S(1)} %fusion.8), channel_id=1, replica_groups=mesh['shard'=64,'tp'=8] {'shard'}, dimensions={0}, use_global_device_ids=true | all-gather | bytes 266240 | tf_op jit(solution)/shard_map/all_gather | solution.py:43
  95.5 0.5 fusion.10
  95.9 1.6 copy.10
  97.5 9.6 %all-to-all-start = ((f32[256,8,128]{2,1,0:T(8,128)}), f32[256,8,128]{2,1,0:T(8,128)S(1)}, u32[]{:S(2)}, u32[]{:S(2)}) async-start(f32[256,8,128]{2,1,0:T(8,128)} %copy.10), calls=%async_computation | async-start | bytes 2097152 | tf_op jit(solution)/shard_map/all_to_all | solution.py:47
  107.2 0.1 reshape.116
  107.3 0.7 gather_fusion.2
  108.0 0.1 reshape.123
  108.1 0.7 gather_fusion.1
  108.8 0.1 reshape.119
  109.0 29.4 %all-to-all-done = f32[256,8,128]{2,1,0:T(8,128)S(1)} async-done(((f32[256,8,128]{2,1,0:T(8,128)}), f32[256,8,128]{2,1,0:T(8,128)S(1)}, u32[]{:S(2)}, u32[]{:S(2)}) %all-to-all-start) | async-done | bytes 1048608 | tf_op jit(solution)/shard_map/all_to_all | solution.py:47
  138.4 33.2 %gather_fusion = f32[4096]{0:T(1024)S(1)} fusion(f32[4,512,128]{2,1,0:T(8,128)S(1)} %bitcast.27, s32[4096]{0:T(1024)S(1)} %or_bitcast_fusion), kind=kCustom, calls=%fused_computation.2 | custom fusion | bytes 81920 | tf_op jit(solution)/shard_map/jit(take_along_axis)/gather | solution.py:50
  171.7 0.1 copy.12
  171.8 0.8 reshape.126
  172.7 51.8 %reduce-scatter.4.cloned.1.call-done = f32[16,32]{1,0:T(8,128)} async-done(((f32[128,32]{1,0:T(8,128)}), f32[16,32]{1,0:T(8,128)}) %reduce-scatter.4.cloned.1.call-update) | async-done | bytes 2064
  224.5 0.8 reshape.127
  225.3 0.7 compare_select_fusion
  (26 shorter events, 0.6 us)
Async XLA Ops:
  6.5 88.9 %copy-start = (bf16[8,128,512]{2,1,0:T(8,128)(2,1)S(1)}, bf16[8,128,512]{2,1,0:T(8,128)(2,1)}, u32[]{:S(2)}) copy-start(bf16[8,128,512]{2,1,0:T(8,128)(2,1)} %param.15) | copy-start | bytes 3145732
  10.5 1.0 copy-start.3
  11.5 19.4 %copy-start.5 = (s32[1,4]{1,0:T(1,128)S(1)}, s32[1,4]{1,0:T(1,128)}, u32[]{:S(2)}) copy-start(s32[1,4]{1,0:T(1,128)} %param.11) | copy-start | bytes 52
  97.5 9.6 %copy-start.4 = (s32[4,8]{1,0:T(4,128)S(1)}, s32[4,8]{1,0:T(4,128)}, u32[]{:S(2)}) copy-start(s32[4,8]{1,0:T(4,128)} %param.12) | copy-start | bytes 388
  97.5 9.7 %copy-start.1 = (s32[512]{0:T(512)S(1)}, s32[512]{0:T(512)}, u32[]{:S(2)}) copy-start(s32[512]{0:T(512)} %param.13) | copy-start | bytes 6148
  97.5 40.8 %all-to-all-start = ((f32[256,8,128]{2,1,0:T(8,128)}), f32[256,8,128]{2,1,0:T(8,128)S(1)}, u32[]{:S(2)}, u32[]{:S(2)}) async-start(f32[256,8,128]{2,1,0:T(8,128)} %copy.10), calls=%async_computation | async-start | bytes 2097152 | tf_op jit(solution)/shard_map/all_to_all | solution.py:47
  107.1 117.4 %reduce-scatter.4.cloned.1.call-start = ((), (), s32[]{:S(2)}) async-start(), calls=%async_computation.2 | async-start | bytes 73728
  107.3 0.8 copy-start.2
Sparse Core Ops, SparseCore 0:
  172.8 51.6 reduce-scatter.3
where the time goes:
time: 234 us; the launch traced here: 233 us
  blocking collectives  83.1 us (36%)
  waiting for transfers between devices  81.2 us (35%)
  local copies, waits for them, and re-layouts  39.2 us (17%)
  between operations  13.5 us (6%)
  starting transfers between devices  9.61 us (4%)
  other arithmetic  3.39 us (1%)
  matrix products  2.88 us (1%)
    all_gather x1, blocking collectives, per_device(): lax.all_gather(query, 'shard', axis=0, tiled=True)  64.4 us
    unnamed x2, waiting for transfers between devices  51.8 us
    gather x1, local copies, waits for them, and re-layouts, per_device(): mine = jnp.take_along_axis(tiles, index, axis=1)  33.2 us
    all_to_all x1, waiting for transfers between devices, per_device(): lax.all_to_all(partial_scores, 'shard', split_axis=0, concat_axis=1, tile...  29.4 us
    psum x1, blocking collectives, per_device(): squares = lax.psum(jnp.sum(pooled * pooled, axis=-1), 'tp')  18.6 us
    all_to_all x1, starting transfers between devices, per_device(): lax.all_to_all(partial_scores, 'shard', split_axis=0, concat_axis=1, tile...  9.57 us
  transfers between devices with their start and end apart: 2, of which 2 were waited for; matrix products, arithmetic and copies ran while one was open for 1% of the time, Pallas kernels for 0%

commit v1 on v0

v1 whole, which is shorter than its diff:
```python
import functools
import math

import jax
import jax.numpy as jnp
from jax import lax
from jax.experimental import pallas as pl
from jax.experimental.pallas import tpu as pltpu
from jax.sharding import PartitionSpec as P

MOST = 4
LANES = 128
VMEM = pl.BlockSpec(memory_space=pltpu.VMEM)
SMEM = pl.BlockSpec(memory_space=pltpu.SMEM)
NT = (((1,), (1,)), ((), ()))


def route(probes_ref, slot_ref, count, local_slots, owners):
    for owner in range(owners):
        count[owner] = 0
    found = []
    requests, nprobe = probes_ref.shape
    for query in range(requests):
        for j in range(nprobe):
            cluster = probes_ref[query, j]
            slot = slot_ref[cluster]
            owner = slot // local_slots
            rank = count[owner]
            count[owner] = rank + 1
            row = owner * MOST + jnp.minimum(rank, MOST - 1)
            found.append((query, query * nprobe + j, cluster, row, slot % local_slots))
    return found


def pool_kernel(local_slots, owners, lens_ref, probes_ref, slot_ref, hid_ref, lat_ref, pay_ref, ss_ref, rows, count):
    tokens, width = hid_ref.shape
    requests = probes_ref.shape[0]
    lat = lat_ref[...]
    scale = 1.0 / math.sqrt(width)
    group = 8
    chunk = 256
    row_id = lax.broadcasted_iota(jnp.int32, (group, chunk), 0)
    position = lax.broadcasted_iota(jnp.int32, (group, chunk), 1)
    begin = jnp.zeros((group, chunk), jnp.int32)
    end = jnp.zeros((group, chunk), jnp.int32)
    length_id = lax.broadcasted_iota(jnp.int32, (group, width), 0)
    length = jnp.ones((group, width), jnp.int32)
    start = jnp.int32(0)
    for r in range(requests):
        n = lens_ref[0, r]
        begin = jnp.where(row_id == r, start, begin)
        end = jnp.where(row_id == r, start + n, end)
        length = jnp.where(length_id == r, n, length)
        start = start + n
    total = jnp.zeros((group, lat.shape[0]), jnp.float32)
    for c in range(tokens // chunk):
        hid = hid_ref[c * chunk : (c + 1) * chunk, :]
        logits = lax.dot_general(lat, hid, NT, preferred_element_type=jnp.float32) * scale
        top = jnp.max(logits, axis=0, keepdims=True)
        e = jnp.exp(logits - top)
        w = (e * (1.0 / jnp.sum(e, axis=0, keepdims=True))).astype(jnp.bfloat16)
        here = position + c * chunk
        member = jnp.where((here >= begin) & (here < end), 1.0, 0.0).astype(jnp.bfloat16)
        total = total + lax.dot_general(member, w, NT, preferred_element_type=jnp.float32)
    hi = total.astype(jnp.bfloat16).astype(jnp.float32)
    rest = total - hi
    mid = rest.astype(jnp.bfloat16).astype(jnp.float32)
    parts = jnp.concatenate([hi, mid, rest - mid, jnp.zeros_like(hi)], axis=0).astype(jnp.bfloat16)
    sums = jnp.dot(parts, lat, preferred_element_type=jnp.float32)
    sums = sums[:group] + sums[group : 2 * group] + sums[2 * group : 3 * group]
    pooled = sums / length.astype(jnp.float32)
    ss_ref[...] = jnp.broadcast_to(jnp.sum(pooled * pooled, axis=1, keepdims=True), ss_ref.shape)
    rows[...] = jnp.zeros_like(rows)
    for query, _, _, row, local in route(probes_ref, slot_ref, count, local_slots, owners):
        mark = jnp.full((1, LANES), local.astype(jnp.float32), jnp.float32)
        rows[pl.ds(row, 1), :] = jnp.concatenate([pooled[query : query + 1, :], mark], axis=1)
    pay_ref[...] = rows[...].astype(jnp.bfloat16)


def score_kernel(local_slots, rows_ref, pas_ref, out_ref):
    width = pas_ref.shape[1]
    cap = out_ref.shape[1]
    rows = rows_ref[:, :width]
    mark = rows_ref[:, width:].astype(jnp.float32)
    total = jnp.zeros(out_ref.shape, jnp.float32)
    for s in range(local_slots):
        got = lax.dot_general(rows, pas_ref[s * cap : (s + 1) * cap, :], NT, preferred_element_type=jnp.float32)
        total = total + jnp.where(mark == float(s), got, 0.0)
    out_ref[...] = total


def pick_kernel(local_slots, owners, probes_ref, slot_ref, size_ref, got_ref, ss_ref, out_ref, buf, count):
    requests, nprobe = probes_ref.shape
    items = requests * nprobe
    lane = lax.broadcasted_iota(jnp.int32, (1, LANES), 1)
    buf[...] = jnp.zeros_like(buf)
    for query, item, cluster, row, _ in route(probes_ref, slot_ref, count, local_slots, owners):
        buf[item : item + 1, :] = jnp.where(lane < size_ref[cluster], got_ref[pl.ds(row, 1), :], 0.0)
    for query in range(requests):
        first = items + query * nprobe
        buf[first : first + nprobe, :] = jnp.broadcast_to(ss_ref[query : query + 1, :], (nprobe, LANES))
    out_ref[...] = buf[...].T.reshape(out_ref.shape)


def finish_kernel(items, got_ref, out_ref, buf):
    cap = got_ref.shape[1]
    buf[...] = jnp.zeros_like(buf)
    total = got_ref[0]
    for t in range(1, got_ref.shape[0]):
        total = total + got_ref[t]
    buf[:cap, :] = total
    turned = buf[...].T
    score = turned[:items, :cap] / jnp.sqrt(turned[items : 2 * items, :cap] + 1e-06)
    out_ref[...] = score.reshape(out_ref.shape)


def per_device(shards, tps, hidden, latents, lengths, probes, cluster_slot, slab_sizes, passages):
    width = hidden.shape[1]
    local_slots, cap, _ = passages.shape
    requests, nprobe = probes.shape
    pack_rows = shards * MOST
    f32 = jnp.float32
    payload, squares = pl.pallas_call(
        functools.partial(pool_kernel, local_slots, shards),
        out_shape=(
            jax.ShapeDtypeStruct((pack_rows, width + LANES), jnp.bfloat16),
            jax.ShapeDtypeStruct((8, LANES), f32),
        ),
        in_specs=[SMEM, SMEM, SMEM, VMEM, VMEM],
        out_specs=(VMEM, VMEM),
        scratch_shapes=[pltpu.VMEM((pack_rows, width + LANES), f32), pltpu.SMEM((shards,), jnp.int32)],
        name="pool",
    )(lengths, probes, cluster_slot, hidden, latents)
    rows = lax.all_to_all(payload.reshape(shards, MOST, width + LANES), "shard", 0, 0, tiled=True)
    scores = pl.pallas_call(
        functools.partial(score_kernel, local_slots),
        out_shape=jax.ShapeDtypeStruct((pack_rows, cap), f32),
        in_specs=[VMEM, VMEM],
        out_specs=VMEM,
        name="score",
    )(rows.reshape(pack_rows, width + LANES), passages.reshape(local_slots * cap, width))
    got = lax.all_to_all(scores.reshape(shards, MOST, cap), "shard", 0, 0, tiled=True)
    picked = pl.pallas_call(
        functools.partial(pick_kernel, local_slots, shards),
        out_shape=jax.ShapeDtypeStruct((tps, cap // tps, LANES), f32),
        in_specs=[SMEM, SMEM, SMEM, VMEM, VMEM],
        out_specs=VMEM,
        scratch_shapes=[pltpu.VMEM((LANES, cap), f32), pltpu.SMEM((shards,), jnp.int32)],
        name="pick",
    )(probes, cluster_slot, slab_sizes, got.reshape(pack_rows, cap), squares)
    parts = lax.all_to_all(picked, "tp", 0, 0, tiled=True)
    return pl.pallas_call(
        functools.partial(finish_kernel, requests * nprobe),
        out_shape=jax.ShapeDtypeStruct((requests, nprobe, cap // tps), f32),
        in_specs=[VMEM],
        out_specs=VMEM,
        scratch_shapes=[pltpu.VMEM((LANES, LANES), f32)],
        name="finish",
    )(parts)


def solution(mesh):
    placed = (
        P("shard", "tp"),
        P(None, "tp"),
        P("shard", None),
        P("shard", None),
        P(),
        P(),
        P("shard", None, "tp"),
    )
    return jax.shard_map(
        functools.partial(per_device, mesh.shape["shard"], mesh.shape["tp"]),
        mesh=mesh,
        in_specs=placed,
        out_specs=P("shard", None, "tp"),
        check_vma=False,
    )
```

time: 234 us -> 86.9 us (0.37)
  waiting for transfers between devices: 81.2 us -> 0 us
  local copies, waits for them, and re-layouts: 39.2 us -> 1.84 us
  between operations: 13.5 us -> 0.01 us
  starting transfers between devices: 9.61 us -> 0 us
  Pallas kernels: 0 us -> 9.34 us
  blocking collectives: 83.1 us -> 75.3 us
  other arithmetic: 3.39 us -> 0 us
  matrix products: 2.88 us -> 0 us
    all_to_all x0 -> x3, blocking collectives: none -> 75.3 us  [the longest x1 40.8 us: per_device(): lax.all_to_all(payload.reshape(shards, MOST, width + LANES), 'shard', 0,...]
    all_gather x1 -> x0, blocking collectives: 64.4 us -> none  [per_device(): lax.all_gather(query, 'shard', axis=0, tiled=True)]
    unnamed x2 -> x0, waiting for transfers between devices: 51.8 us -> none
    gather x5 -> x0, local copies, waits for them, and re-layouts: 34.8 us -> none  [the longest x1 33.2 us: per_device(): mine = jnp.take_along_axis(tiles, index, axis=1)]
    all_to_all x1 -> x0, waiting for transfers between devices: 29.4 us -> none  [per_device(): lax.all_to_all(partial_scores, 'shard', split_axis=0, concat_axis=1, tile...]
    psum x1 -> x0, blocking collectives: 18.6 us -> none  [per_device(): squares = lax.psum(jnp.sum(pooled * pooled, axis=-1), 'tp')]
    all_to_all x1 -> x0, starting transfers between devices: 9.57 us -> none  [per_device(): lax.all_to_all(partial_scores, 'shard', split_axis=0, concat_axis=1, tile...]
    pallas_call x0 -> x4, Pallas kernels: none -> 9.34 us  [the longest x1 3.19 us: per_device(): pl.pallas_call(functools.partial(pool_kernel, local_slots, shards), out_s...]
  transfers between devices with their start and end apart: 2 -> 0, of which waited for: 2 -> 0; matrix products, arithmetic and copies ran while one was open for 1% -> 0% of each run, Pallas kernels for 0% -> 0%
where the time goes in v1:
time: 86.9 us; the launch traced here: 86.5 us
  blocking collectives  75.3 us (87%)
  Pallas kernels  9.34 us (11%)
  local copies, waits for them, and re-layouts  1.84 us (2%)
    all_to_all x1, blocking collectives, per_device(): lax.all_to_all(payload.reshape(shards, MOST, width + LANES), 'shard', 0,...  40.8 us
    all_to_all x1, blocking collectives, per_device(): lax.all_to_all(scores.reshape(shards, MOST, cap), 'shard', 0, 0, tiled=True)  21.7 us
    all_to_all x1, blocking collectives, per_device(): parts = lax.all_to_all(picked, 'tp', 0, 0, tiled=True)  12.8 us
    pallas_call x1, Pallas kernels, per_device(): pl.pallas_call(functools.partial(pool_kernel, local_slots, shards), out_s...  3.19 us
    pallas_call x1, Pallas kernels, per_device(): pl.pallas_call(functools.partial(score_kernel, local_slots), out_shape=ja...  2.69 us
    pallas_call x1, Pallas kernels, per_device(): pl.pallas_call(functools.partial(pick_kernel, local_slots, shards), out_s...  1.92 us

profile of v1, /device:TPU:1, one launch (start us, length us, event | category | flops | bytes accessed | tf_op | source)
XLA Modules:
  0.0 86.5 jit_solution(9818761524487508846)
XLA Ops:
  0.0 3.2 %pool.1 = (bf16[256,640]{1,0:T(8,128)(2,1)}, f32[8,128]{1,0:T(8,128)}) custom-call(s32[1,4]{1,0:T(1,128)} %lens_ref.1, s32[4,8]{1,0:T(4,128)} %probes_ref.3, s32[512]{0:T(512)} %slot_ref.3, bf16[512,512]{1,0:T(8,128)(2,1)} %hid_ref.1, bf16[512,512]{1,0:T(8,128)(2,1)} %lat_ref.1), custom_call_target="tpu_custom_call" | custom-call | tf_op jit(solution)/shard_map/pool/pallas_call | solution.py:123
  3.2 1.1 %reshape.15 = bf16[64,4,640]{2,1,0:T(4,128)(2,1)S(1)} reshape(bf16[256,640]{1,0:T(8,128)(2,1)} %get-tuple-element.7) | data formatting | bytes 655360 | tf_op jit(solution)/shard_map/reshape | solution.py:134
  4.2 40.8 %all_to_all.15 = bf16[64,4,640]{2,1,0:T(4,128)(2,1)S(1)} all-to-all(bf16[64,4,640]{2,1,0:T(4,128)(2,1)S(1)} %reshape.15), channel_id=1, replica_groups=mesh['shard'=64,'tp'=8] {'shard'}, dimensions={0} | all-to-all | bytes 655360 | tf_op jit(solution)/shard_map/all_to_all | solution.py:134
  45.0 0.8 reshape.16.rows_ref
  45.8 2.7 %score.1 = f32[256,128]{1,0:T(8,128)} custom-call(bf16[256,640]{1,0:T(8,128)(2,1)} %reshape.16.rows_ref, bf16[1024,512]{1,0:T(8,128)(2,1)} %bitcast.3), custom_call_target="tpu_custom_call" | custom-call | tf_op jit(solution)/shard_map/score/pallas_call | solution.py:135
  48.5 21.7 %all_to_all.16 = f32[64,4,128]{2,1,0:T(4,128)} all-to-all(f32[64,4,128]{2,1,0:T(4,128)} %bitcast.4), channel_id=1, replica_groups=mesh['shard'=64,'tp'=8] {'shard'}, dimensions={0} | all-to-all | bytes 262144 | tf_op jit(solution)/shard_map/all_to_all | solution.py:142
  70.2 1.9 %pick.1 = f32[8,16,128]{2,1,0:T(8,128)} custom-call(s32[4,8]{1,0:T(4,128)} %probes_ref.3, s32[512]{0:T(512)} %slot_ref.3, s32[512]{0:T(512)} %size_ref.1, f32[256,128]{1,0:T(8,128)} %bitcast.5, f32[8,128]{1,0:T(8,128)} %get-tuple-element.8.ss_ref), custom_call_target="tpu_custom_call" | custom-call | tf_op jit(solution)/shard_map/pick/pallas_call | solution.py:143
  72.1 12.8 %all_to_all.17.got_ref = f32[8,16,128]{2,1,0:T(8,128)} all-to-all(f32[8,16,128]{2,1,0:T(8,128)} %pick.1), channel_id=1, replica_groups=mesh['shard'=64,'tp'=8] {'tp'}, dimensions={0} | all-to-all | bytes 131072 | tf_op jit(solution)/shard_map/all_to_all | solution.py:151
  84.9 1.6 %finish.1 = f32[4,8,16]{2,1,0:T(8,128)} custom-call(f32[8,16,128]{2,1,0:T(8,128)} %all_to_all.17.got_ref), custom_call_target="tpu_custom_call" | custom-call | tf_op jit(solution)/shard_map/finish/pallas_call | solution.py:152

commit v2 on v1

v2 whole, which is shorter than its diff:
```python
import functools
import math

import jax
import jax.numpy as jnp
from jax import lax
from jax.experimental import pallas as pl
from jax.experimental.pallas import tpu as pltpu
from jax.sharding import PartitionSpec as P

MOST = 4
LANES = 128
VMEM = pl.BlockSpec(memory_space=pltpu.VMEM)
SMEM = pl.BlockSpec(memory_space=pltpu.SMEM)
NT = (((1,), (1,)), ((), ()))


def pool_kernel(
    local_slots, owners, lens_ref, probes_ref, slot_ref, size_ref, hid_ref, lat_ref,
    pay_ref, ss_ref, route_ref, rows, count,
):
    tokens, width = hid_ref.shape
    requests, nprobe = probes_ref.shape
    pieces = width // LANES
    block = MOST * pieces + MOST // 2
    for owner in range(owners):
        count[owner] = 0
    rows[...] = jnp.zeros_like(rows)
    lane = lax.broadcasted_iota(jnp.int32, (1, LANES), 1)
    places = []
    for query in range(requests):
        for j in range(nprobe):
            cluster = probes_ref[query, j]
            slot = slot_ref[cluster]
            owner = slot // local_slots
            rank = jnp.minimum(count[owner], MOST - 1)
            count[owner] = rank + 1
            route_ref[0, query * nprobe + j] = owner * MOST + rank
            route_ref[1, query * nprobe + j] = size_ref[cluster]
            mark = owner * block + MOST * pieces + rank // 2
            side = (lane // (LANES // 2)) == rank % 2
            local = (slot % local_slots).astype(jnp.float32)
            rows[pl.ds(mark, 1), :] = jnp.where(side, local, rows[pl.ds(mark, 1), :])
            places.append((query, owner * block + rank * pieces))
    lat = lat_ref[...]
    scale = 1.0 / math.sqrt(width)
    group = 8
    chunk = 256
    row_id = lax.broadcasted_iota(jnp.int32, (group, chunk), 0)
    position = lax.broadcasted_iota(jnp.int32, (group, chunk), 1)
    begin = jnp.zeros((group, chunk), jnp.int32)
    end = jnp.zeros((group, chunk), jnp.int32)
    length_id = lax.broadcasted_iota(jnp.int32, (group, width), 0)
    length = jnp.ones((group, width), jnp.int32)
    start = jnp.int32(0)
    for r in range(requests):
        n = lens_ref[0, r]
        begin = jnp.where(row_id == r, start, begin)
        end = jnp.where(row_id == r, start + n, end)
        length = jnp.where(length_id == r, n, length)
        start = start + n
    total = jnp.zeros((group, lat.shape[0]), jnp.float32)
    for c in range(tokens // chunk):
        hid = hid_ref[c * chunk : (c + 1) * chunk, :]
        logits = lax.dot_general(lat, hid, NT, preferred_element_type=jnp.float32) * scale
        top = jnp.max(logits, axis=0, keepdims=True)
        e = jnp.exp(logits - top)
        w = (e * (1.0 / jnp.sum(e, axis=0, keepdims=True))).astype(jnp.bfloat16)
        here = position + c * chunk
        member = jnp.where((here >= begin) & (here < end), 1.0, 0.0).astype(jnp.bfloat16)
        total = total + lax.dot_general(member, w, NT, preferred_element_type=jnp.float32)
    hi = total.astype(jnp.bfloat16).astype(jnp.float32)
    rest = total - hi
    mid = rest.astype(jnp.bfloat16).astype(jnp.float32)
    parts = jnp.concatenate([hi, mid, rest - mid, jnp.zeros_like(hi)], axis=0).astype(jnp.bfloat16)
    sums = jnp.dot(parts, lat, preferred_element_type=jnp.float32)
    sums = sums[:group] + sums[group : 2 * group] + sums[2 * group : 3 * group]
    pooled = sums / length.astype(jnp.float32)
    ss_ref[...] = jnp.broadcast_to(jnp.sum(pooled * pooled, axis=1, keepdims=True), ss_ref.shape)
    for query, place in places:
        for f in range(pieces):
            rows[pl.ds(place + f, 1), :] = pooled[query : query + 1, f * LANES : (f + 1) * LANES]
    pay_ref[...] = rows[...].astype(jnp.bfloat16)


def score_kernel(local_slots, owners, rows_ref, pas_ref, out_ref, rows):
    cap = out_ref.shape[1]
    pieces = pas_ref.shape[1] // LANES
    block = rows_ref.shape[0] // owners
    rows[...] = rows_ref[...].astype(jnp.float32)
    lane = lax.broadcasted_iota(jnp.int32, (owners, LANES), 1)
    query = []
    mark = []
    for k in range(MOST):
        piece = [rows[pl.ds(k * pieces + f, owners, stride=block), :] for f in range(pieces)]
        query.append(jnp.concatenate(piece, axis=1))
        own = rows[pl.ds(MOST * pieces + k // 2, owners, stride=block), :]
        side = (lane // (LANES // 2)) == k % 2
        mark.append(jnp.where(side, own, pltpu.roll(own, LANES // 2, 1)))
    query = jnp.concatenate(query, axis=0).astype(jnp.bfloat16)
    mark = jnp.concatenate(mark, axis=0)
    total = jnp.zeros(out_ref.shape, jnp.float32)
    for s in range(local_slots):
        got = lax.dot_general(query, pas_ref[s * cap : (s + 1) * cap, :], NT, preferred_element_type=jnp.float32)
        total = total + jnp.where(mark == float(s), got, 0.0)
    for k in range(MOST):
        out_ref[pl.ds(k, owners, stride=MOST), :] = total[k * owners : (k + 1) * owners]


def pick_kernel(requests, route_ref, got_ref, ss_ref, out_ref, buf):
    items = route_ref.shape[1]
    nprobe = items // requests
    lane = lax.broadcasted_iota(jnp.int32, (1, LANES), 1)
    buf[2 * items :, :] = jnp.zeros((LANES - 2 * items, buf.shape[1]), jnp.float32)
    for item in range(items):
        buf[item : item + 1, :] = jnp.where(lane < route_ref[1, item], got_ref[pl.ds(route_ref[0, item], 1), :], 0.0)
    for query in range(requests):
        first = items + query * nprobe
        buf[first : first + nprobe, :] = jnp.broadcast_to(ss_ref[query : query + 1, :], (nprobe, LANES))
    out_ref[...] = buf[...].T.reshape(out_ref.shape)


def finish_kernel(items, got_ref, out_ref, buf):
    cap = got_ref.shape[1]
    buf[cap:, :] = jnp.zeros((LANES - cap, LANES), jnp.float32)
    total = got_ref[0]
    for t in range(1, got_ref.shape[0]):
        total = total + got_ref[t]
    buf[:cap, :] = total
    turned = buf[...].T
    score = turned[:items, :cap] / jnp.sqrt(turned[items : 2 * items, :cap] + 1e-06)
    out_ref[...] = score.reshape(out_ref.shape)


def pool(local_slots, owners, lengths, probes, cluster_slot, slab_sizes, hidden, latents):
    width = hidden.shape[1]
    block = MOST * (width // LANES) + MOST // 2
    f32 = jnp.float32
    return pl.pallas_call(
        functools.partial(pool_kernel, local_slots, owners),
        out_shape=(
            jax.ShapeDtypeStruct((owners * block, LANES), jnp.bfloat16),
            jax.ShapeDtypeStruct((8, LANES), f32),
            jax.ShapeDtypeStruct((2, probes.size), jnp.int32),
        ),
        in_specs=[SMEM, SMEM, SMEM, SMEM, VMEM, VMEM],
        out_specs=(VMEM, VMEM, SMEM),
        scratch_shapes=[pltpu.VMEM((owners * block, LANES), f32), pltpu.SMEM((owners,), jnp.int32)],
        name="pool",
    )(lengths, probes, cluster_slot, slab_sizes, hidden, latents)


def score(owners, rows, passages):
    local_slots, cap, width = passages.shape
    return pl.pallas_call(
        functools.partial(score_kernel, local_slots, owners),
        out_shape=jax.ShapeDtypeStruct((owners * MOST, cap), jnp.float32),
        in_specs=[VMEM, VMEM],
        out_specs=VMEM,
        scratch_shapes=[pltpu.VMEM(rows.shape, jnp.float32)],
        name="score",
    )(rows, passages.reshape(local_slots * cap, width))


def pick(tps, requests, route, got, squares):
    cap = got.shape[1]
    return pl.pallas_call(
        functools.partial(pick_kernel, requests),
        out_shape=jax.ShapeDtypeStruct((tps, cap // tps, LANES), jnp.float32),
        in_specs=[SMEM, VMEM, VMEM],
        out_specs=VMEM,
        scratch_shapes=[pltpu.VMEM((LANES, cap), jnp.float32)],
        name="pick",
    )(route, got, squares)


def finish(requests, nprobe, parts):
    return pl.pallas_call(
        functools.partial(finish_kernel, requests * nprobe),
        out_shape=jax.ShapeDtypeStruct((requests, nprobe, parts.shape[1]), jnp.float32),
        in_specs=[VMEM],
        out_specs=VMEM,
        scratch_shapes=[pltpu.VMEM((LANES, LANES), jnp.float32)],
        name="finish",
    )(parts)


def per_device(shards, tps, hidden, latents, lengths, probes, cluster_slot, slab_sizes, passages):
    local_slots, cap, _ = passages.shape
    requests, nprobe = probes.shape
    payload, squares, route = pool(
        local_slots, shards, lengths, probes, cluster_slot, slab_sizes, hidden, latents
    )
    blocks = payload.reshape(shards, -1, 2, LANES)
    rows = lax.all_to_all(blocks, "shard", 0, 0, tiled=True).reshape(payload.shape)
    scores = score(shards, rows, passages)
    got = lax.all_to_all(scores.reshape(shards, 1, MOST * cap), "shard", 0, 0, tiled=True)
    picked = pick(tps, requests, route, got.reshape(scores.shape), squares)
    parts = lax.all_to_all(picked, "tp", 0, 0, tiled=True)
    return finish(requests, nprobe, parts)


def solution(mesh):
    placed = (
        P("shard", "tp"),
        P(None, "tp"),
        P("shard", None),
        P("shard", None),
        P(),
        P(),
        P("shard", None, "tp"),
    )
    return jax.shard_map(
        functools.partial(per_device, mesh.shape["shard"], mesh.shape["tp"]),
        mesh=mesh,
        in_specs=placed,
        out_specs=P("shard", None, "tp"),
        check_vma=False,
    )
```

time: 86.9 us -> 83.8 us (0.964)
  local copies, waits for them, and re-layouts: 1.84 us -> 0 us
  blocking collectives: 75.3 us -> 74.1 us
    reshape x2 -> x0, local copies, waits for them, and re-layouts: 1.84 us -> none  [the longest x1 1.05 us: per_device(): payload.reshape(shards, MOST, width + LANES)]
    all_to_all x2, blocking collectives: 62.5 us -> 61.4 us  [the longest x1 39.3 us: per_device(): lax.all_to_all(blocks, 'shard', 0, 0, tiled=True).reshape(payload.shape)]
where the time goes in v2:
time: 83.8 us; the launch traced here: 83.4 us
  blocking collectives  74.1 us (88%)
  Pallas kernels  9.3 us (11%)
    all_to_all x1, blocking collectives, per_device(): lax.all_to_all(blocks, 'shard', 0, 0, tiled=True).reshape(payload.shape)  39.3 us
    all_to_all x1, blocking collectives, per_device(): lax.all_to_all(scores.reshape(shards, 1, MOST * cap), 'shard', 0, 0, tile...  22.1 us
    all_to_all x1, blocking collectives, per_device(): parts = lax.all_to_all(picked, 'tp', 0, 0, tiled=True)  12.7 us
    pallas_call x1, Pallas kernels, pool(): pl.pallas_call(functools.partial(pool_kernel, local_slots, owners), out_s...  3.37 us
    pallas_call x1, Pallas kernels, score(): pl.pallas_call(functools.partial(score_kernel, local_slots, owners), out_...  2.69 us
    pallas_call x1, Pallas kernels, pick(): pl.pallas_call(functools.partial(pick_kernel, requests), out_shape=jax.Sh...  1.68 us

profile of v2, /device:TPU:1, one launch (start us, length us, event | category | flops | bytes accessed | tf_op | source)
XLA Modules:
  0.0 83.4 jit_solution(6468934139422224413)
XLA Ops:
  0.0 3.4 %pool.1 = (bf16[1152,128]{1,0:T(8,128)(2,1)}, f32[8,128]{1,0:T(8,128)}, s32[2,32]{1,0:T(2,128)}) custom-call(s32[1,4]{1,0:T(1,128)} %lens_ref.1, s32[4,8]{1,0:T(4,128)} %probes_ref.1, s32[512]{0:T(512)} %slot_ref.1, s32[512]{0:T(512)} %size_ref.1, bf16[512,512]{1,0:T(8,128)(2,1)} %hid_ref.1, bf16[512,512]{1,0:T(8,128)(2,1)} %lat_ref.1), custom_call_target="tpu_custom_call" | custom-call | tf_op jit(solution)/shard_map/pool/pallas_call | solution.py:139
  3.4 39.3 %all_to_all.15 = bf16[64,9,2,128]{3,2,1,0:T(2,128)(2,1)} all-to-all(bf16[64,9,2,128]{3,2,1,0:T(2,128)(2,1)} %bitcast.9), channel_id=1, replica_groups=mesh['shard'=64,'tp'=8] {'shard'}, dimensions={0} | all-to-all | bytes 589824 | tf_op jit(solution)/shard_map/all_to_all | solution.py:195
  42.6 2.7 %score.1 = f32[256,128]{1,0:T(8,128)} custom-call(bf16[1152,128]{1,0:T(8,128)(2,1)} %bitcast.5, bf16[1024,512]{1,0:T(8,128)(2,1)} %bitcast.6), custom_call_target="tpu_custom_call" | custom-call | tf_op jit(solution)/shard_map/score/pallas_call | solution.py:155
  45.3 22.1 %all_to_all.16 = f32[64,1,512]{2,1,0:T(1,128)} all-to-all(f32[64,1,512]{2,1,0:T(1,128)} %bitcast.7), channel_id=1, replica_groups=mesh['shard'=64,'tp'=8] {'shard'}, dimensions={0} | all-to-all | bytes 262144 | tf_op jit(solution)/shard_map/all_to_all | solution.py:197
  67.4 1.7 %pick.1 = f32[8,16,128]{2,1,0:T(8,128)} custom-call(s32[2,32]{1,0:T(2,128)} %get-tuple-element.8.route_ref, f32[256,128]{1,0:T(8,128)} %bitcast.8, f32[8,128]{1,0:T(8,128)} %get-tuple-element.10.ss_ref), custom_call_target="tpu_custom_call" | custom-call | tf_op jit(solution)/shard_map/pick/pallas_call | solution.py:167
  69.1 12.7 %all_to_all.17.got_ref = f32[8,16,128]{2,1,0:T(8,128)} all-to-all(f32[8,16,128]{2,1,0:T(8,128)} %pick.1), channel_id=1, replica_groups=mesh['shard'=64,'tp'=8] {'tp'}, dimensions={0} | all-to-all | bytes 131072 | tf_op jit(solution)/shard_map/all_to_all | solution.py:199
  81.8 1.6 %finish.1 = f32[4,8,16]{2,1,0:T(8,128)} custom-call(f32[8,16,128]{2,1,0:T(8,128)} %all_to_all.17.got_ref), custom_call_target="tpu_custom_call" | custom-call | tf_op jit(solution)/shard_map/finish/pallas_call | solution.py:178

commit v3 on v2

v3 whole, which is shorter than its diff:
```python
import functools
import math

import jax
import jax.numpy as jnp
from jax import lax
from jax.experimental import pallas as pl
from jax.experimental.pallas import tpu as pltpu
from jax.sharding import PartitionSpec as P

MOST = 4
LANES = 128
GROUP = 8
VMEM = pl.BlockSpec(memory_space=pltpu.VMEM)
SMEM = pl.BlockSpec(memory_space=pltpu.SMEM)
HBM = pl.BlockSpec(memory_space=pltpu.HBM)
NT = (((1,), (1,)), ((), ()))
PARAMS = pltpu.CompilerParams(vmem_limit_bytes=16 << 20)


def pool_kernel(
    local_slots, owners, lens_hbm, probes_hbm, slot_hbm, size_hbm, hid_hbm, lat_hbm,
    pay_ref, ss_ref, route_ref,
    halves, count, code, lens_ref, probes_ref, slot_ref, size_ref, hid_ref, lat_ref, sems,
):
    tokens, width = hid_ref.shape
    requests, nprobe = probes_ref.shape
    pieces = width // LANES
    pairs = pieces // 2
    bits = local_slots.bit_length() - 1
    copies = [
        pltpu.make_async_copy(source, target, sems.at[i])
        for i, (source, target) in enumerate(
            [
                (probes_hbm, probes_ref),
                (slot_hbm, slot_ref),
                (lens_hbm, lens_ref),
                (size_hbm, size_ref),
                (lat_hbm, lat_ref),
                (hid_hbm, hid_ref),
            ]
        )
    ]
    for copy in copies:
        copy.start()
    for owner in range(owners):
        count[owner] = 0
        code[owner] = 0
    pay_ref[...] = jnp.zeros_like(pay_ref)
    for copy in copies:
        copy.wait()

    places = []
    for query in range(requests):
        for j in range(nprobe):
            item = query * nprobe + j
            cluster = probes_ref[query, j]
            slot = slot_ref[cluster]
            owner = lax.shift_right_logical(slot, bits)
            rank = jnp.minimum(count[owner], MOST - 1)
            count[owner] = rank + 1
            code[owner] = code[owner] | ((slot & (local_slots - 1)) << (bits * rank))
            route_ref[0, item] = owner * MOST + rank
            route_ref[1, item] = size_ref[cluster]
            places.append((query, owner, rank))
    side = lax.broadcasted_iota(jnp.int32, (2, LANES), 0)
    half = bits * MOST // 2
    for _, owner, _ in places:
        both = code[owner]
        mark = jnp.where(side == 0, both & ((1 << half) - 1), lax.shift_right_logical(both, half))
        pay_ref[owner, MOST * pairs] = mark.astype(jnp.float32).astype(jnp.bfloat16)

    row_id = lax.broadcasted_iota(jnp.int32, (GROUP, tokens), 0)
    position = lax.broadcasted_iota(jnp.int32, (GROUP, tokens), 1)
    begin = jnp.zeros((GROUP, tokens), jnp.int32)
    end = jnp.zeros((GROUP, tokens), jnp.int32)
    length_id = lax.broadcasted_iota(jnp.int32, (GROUP, width), 0)
    length = jnp.ones((GROUP, width), jnp.int32)
    start = jnp.int32(0)
    for r in range(requests):
        n = lens_ref[0, r]
        begin = jnp.where(row_id == r, start, begin)
        end = jnp.where(row_id == r, start + n, end)
        length = jnp.where(length_id == r, n, length)
        start = start + n
    member = jnp.where((position >= begin) & (position < end), 1.0, 0.0).astype(jnp.bfloat16)
    lat = lat_ref[...]
    logits = lax.dot_general(hid_ref[...], lat, NT, preferred_element_type=jnp.float32)
    top = jnp.max(logits, axis=1, keepdims=True)
    e = jnp.exp2((logits - top) * (math.log2(math.e) / math.sqrt(width)))
    weights = (e * (1.0 / jnp.sum(e, axis=1, keepdims=True))).astype(jnp.bfloat16)
    total = jnp.dot(member, weights, preferred_element_type=jnp.float32)
    hi = total.astype(jnp.bfloat16).astype(jnp.float32)
    rest = total - hi
    mid = rest.astype(jnp.bfloat16).astype(jnp.float32)
    parts = jnp.concatenate([hi, mid, rest - mid, jnp.zeros_like(hi)], axis=0).astype(jnp.bfloat16)
    sums = jnp.dot(parts, lat, preferred_element_type=jnp.float32)
    sums = sums[:GROUP] + sums[GROUP : 2 * GROUP] + sums[2 * GROUP : 3 * GROUP]
    pooled = sums / length.astype(jnp.float32)
    ss_ref[...] = jnp.broadcast_to(jnp.sum(pooled * pooled, axis=1, keepdims=True), ss_ref.shape)

    for query in range(requests):
        for f in range(pieces):
            halves[query * pairs + f // 2, f % 2 : f % 2 + 1, :] = pooled[
                query : query + 1, f * LANES : (f + 1) * LANES
            ]
    row = [halves[q * pairs : (q + 1) * pairs].astype(jnp.bfloat16) for q in range(requests)]
    for query, owner, rank in places:
        pay_ref[owner, pl.ds(rank * pairs, pairs)] = row[query]


def score_kernel(local_slots, owners, rows_ref, pas_ref, out_ref, rows):
    cap = out_ref.shape[1]
    pieces = pas_ref.shape[1] // LANES
    block = rows_ref.shape[0] // owners
    bits = local_slots.bit_length() - 1
    rows[...] = rows_ref[...].astype(jnp.float32)
    query = []
    local = []
    for k in range(MOST):
        piece = [rows[pl.ds(k * pieces + f, owners, stride=block), :] for f in range(pieces)]
        query.append(jnp.concatenate(piece, axis=1))
        mark = rows[pl.ds(MOST * pieces + k // 2, owners, stride=block), :].astype(jnp.int32)
        local.append(lax.shift_right_logical(mark, bits * (k % 2)) & (local_slots - 1))
    query = jnp.concatenate(query, axis=0).astype(jnp.bfloat16)
    local = jnp.concatenate(local, axis=0)
    total = jnp.zeros(out_ref.shape, jnp.float32)
    for s in range(local_slots):
        got = lax.dot_general(query, pas_ref[s * cap : (s + 1) * cap, :], NT, preferred_element_type=jnp.float32)
        total = total + jnp.where(local == s, got, 0.0)
    for k in range(MOST):
        out_ref[pl.ds(k, owners, stride=MOST), :] = total[k * owners : (k + 1) * owners]


def pick_kernel(requests, route_ref, got_ref, ss_ref, out_ref, buf):
    items = route_ref.shape[1]
    nprobe = items // requests
    lane = lax.broadcasted_iota(jnp.int32, (1, LANES), 1)
    buf[2 * items :, :] = jnp.zeros((LANES - 2 * items, buf.shape[1]), jnp.float32)
    for item in range(items):
        row = got_ref[pl.ds(route_ref[0, item], 1), :]
        buf[item : item + 1, :] = jnp.where(lane < route_ref[1, item], row, 0.0)
    for query in range(requests):
        first = items + query * nprobe
        buf[first : first + nprobe, :] = jnp.broadcast_to(ss_ref[query : query + 1, :], (nprobe, LANES))
    out_ref[...] = buf[...].T.reshape(out_ref.shape)


def finish_kernel(items, got_ref, out_ref, buf):
    cap = got_ref.shape[1]
    buf[cap:, :] = jnp.zeros((LANES - cap, LANES), jnp.float32)
    total = got_ref[0]
    for t in range(1, got_ref.shape[0]):
        total = total + got_ref[t]
    buf[:cap, :] = total
    turned = buf[...].T
    score = turned[:items, :cap] / jnp.sqrt(turned[items : 2 * items, :cap] + 1e-06)
    out_ref[...] = score.reshape(out_ref.shape)


def pool(local_slots, owners, lengths, probes, cluster_slot, slab_sizes, hidden, latents):
    pairs = hidden.shape[1] // LANES // 2
    whole = jnp.int32
    operands = (lengths, probes, cluster_slot, slab_sizes, hidden, latents)
    return pl.pallas_call(
        functools.partial(pool_kernel, local_slots, owners),
        out_shape=(
            jax.ShapeDtypeStruct((owners, MOST * pairs + 1, 2, LANES), jnp.bfloat16),
            jax.ShapeDtypeStruct((GROUP, LANES), jnp.float32),
            jax.ShapeDtypeStruct((2, probes.size), whole),
        ),
        in_specs=[HBM] * len(operands),
        out_specs=(VMEM, VMEM, SMEM),
        scratch_shapes=[
            pltpu.VMEM((probes.shape[0] * pairs, 2, LANES), jnp.float32),
            pltpu.SMEM((owners,), whole),
            pltpu.SMEM((owners,), whole),
            pltpu.SMEM(lengths.shape, whole),
            pltpu.SMEM(probes.shape, whole),
            pltpu.SMEM(cluster_slot.shape, whole),
            pltpu.SMEM(slab_sizes.shape, whole),
            pltpu.VMEM(hidden.shape, hidden.dtype),
            pltpu.VMEM(latents.shape, latents.dtype),
            pltpu.SemaphoreType.DMA((len(operands),)),
        ],
        name="pool",
        compiler_params=PARAMS,
    )(*(pltpu.with_memory_space_constraint(x, pltpu.HBM) for x in operands))


def score(owners, rows, passages):
    local_slots, cap, width = passages.shape
    return pl.pallas_call(
        functools.partial(score_kernel, local_slots, owners),
        out_shape=jax.ShapeDtypeStruct((owners * MOST, cap), jnp.float32),
        in_specs=[VMEM, VMEM],
        out_specs=VMEM,
        scratch_shapes=[pltpu.VMEM(rows.shape, jnp.float32)],
        name="score",
        compiler_params=PARAMS,
    )(rows, passages.reshape(local_slots * cap, width))


def pick(tps, requests, route, got, squares):
    cap = got.shape[1]
    return pl.pallas_call(
        functools.partial(pick_kernel, requests),
        out_shape=jax.ShapeDtypeStruct((tps, cap // tps, LANES), jnp.float32),
        in_specs=[SMEM, VMEM, VMEM],
        out_specs=VMEM,
        scratch_shapes=[pltpu.VMEM((LANES, cap), jnp.float32)],
        name="pick",
        compiler_params=PARAMS,
    )(route, got, squares)


def finish(requests, nprobe, parts):
    return pl.pallas_call(
        functools.partial(finish_kernel, requests * nprobe),
        out_shape=jax.ShapeDtypeStruct((requests, nprobe, parts.shape[1]), jnp.float32),
        in_specs=[VMEM],
        out_specs=VMEM,
        scratch_shapes=[pltpu.VMEM((LANES, LANES), jnp.float32)],
        name="finish",
        compiler_params=PARAMS,
    )(parts)


def per_device(shards, tps, hidden, latents, lengths, probes, cluster_slot, slab_sizes, passages):
    local_slots, cap, _ = passages.shape
    requests, nprobe = probes.shape
    payload, squares, route = pool(
        local_slots, shards, lengths, probes, cluster_slot, slab_sizes, hidden, latents
    )
    rows = lax.all_to_all(payload, "shard", 0, 0, tiled=True)
    scores = score(shards, rows.reshape(-1, LANES), passages)
    got = lax.all_to_all(scores.reshape(shards, 1, MOST * cap), "shard", 0, 0, tiled=True)
    picked = pick(tps, requests, route, got.reshape(scores.shape), squares)
    parts = lax.all_to_all(picked, "tp", 0, 0, tiled=True)
    return finish(requests, nprobe, parts)


def solution(mesh):
    placed = (
        P("shard", "tp"),
        P(None, "tp"),
        P("shard", None),
        P("shard", None),
        P(),
        P(),
        P("shard", None, "tp"),
    )
    return jax.shard_map(
        functools.partial(per_device, mesh.shape["shard"], mesh.shape["tp"]),
        mesh=mesh,
        in_specs=placed,
        out_specs=P("shard", None, "tp"),
        check_vma=False,
    )
```

time: 83.8 us -> 78.4 us (0.936)
  Pallas kernels: 9.3 us -> 5.06 us
  blocking collectives: 74.1 us -> 73.1 us
    pallas_call x1, Pallas kernels: 2.69 us -> 0.72 us  [score(): pl.pallas_call(functools.partial(score_kernel, local_slots, owners), out_...]
    pallas_call x1, Pallas kernels: 1.68 us -> 0.67 us  [pick(): pl.pallas_call(functools.partial(pick_kernel, requests), out_shape=jax.Sh...]
    pallas_call x1, Pallas kernels: 1.55 us -> 0.71 us  [finish(): pl.pallas_call(functools.partial(finish_kernel, requests * nprobe), out_s...]
where the time goes in v3:
time: 78.4 us; the launch traced here: 78.2 us
  blocking collectives  73.1 us (93%)
  Pallas kernels  5.06 us (6%)
    all_to_all x1, blocking collectives, per_device(): rows = lax.all_to_all(payload, 'shard', 0, 0, tiled=True)  38.9 us
    all_to_all x1, blocking collectives, per_device(): lax.all_to_all(scores.reshape(shards, 1, MOST * cap), 'shard', 0, 0, tile...  21.8 us
    all_to_all x1, blocking collectives, per_device(): parts = lax.all_to_all(picked, 'tp', 0, 0, tiled=True)  12.4 us
    pallas_call x1, Pallas kernels, pool(): pl.pallas_call(functools.partial(pool_kernel, local_slots, owners), out_s...  2.96 us

profile of v3, /device:TPU:1, one launch (start us, length us, event | category | flops | bytes accessed | tf_op | source)
XLA Modules:
  0.0 78.2 jit_solution(11285293930784057078)
XLA Ops:
  0.0 0.0 copy-start
  0.0 3.0 %pool.1 = (bf16[64,9,2,128]{3,2,1,0:T(2,128)(2,1)S(1)}, f32[8,128]{1,0:T(8,128)S(1)}, s32[2,32]{1,0:T(2,128)S(1)}) custom-call(s32[1,4]{1,0:T(1,128)} %lens_hbm.1, s32[4,8]{1,0:T(4,128)} %probes_hbm.1, s32[512]{0:T(512)} %slot_hbm.1, s32[512]{0:T(512)} %size_hbm.1, bf16[512,512]{1,0:T(8,128)(2,1)} %hid_hbm.1, bf16[512,512]{1,0:T(8,128)(2,1)} %lat_hbm.1), custom_call_target="tpu_custom_call" | custom-call | tf_op jit(solution)/shard_map/pool/pallas_call | solution.py:165
  3.0 38.9 %all_to_all.15 = bf16[64,9,2,128]{3,2,1,0:T(2,128)(2,1)S(1)} all-to-all(bf16[64,9,2,128]{3,2,1,0:T(2,128)(2,1)S(1)} %get-tuple-element.9), channel_id=1, replica_groups=mesh['shard'=64,'tp'=8] {'shard'}, dimensions={0} | all-to-all | bytes 589824 | tf_op jit(solution)/shard_map/all_to_all | solution.py:235
  41.9 0.0 copy-done
  41.9 0.7 score.1
  42.6 21.8 %all_to_all.16 = f32[64,1,512]{2,1,0:T(1,128)S(1)} all-to-all(f32[64,1,512]{2,1,0:T(1,128)S(1)} %bitcast.6), channel_id=1, replica_groups=mesh['shard'=64,'tp'=8] {'shard'}, dimensions={0} | all-to-all | bytes 262144 | tf_op jit(solution)/shard_map/all_to_all | solution.py:237
  64.5 0.7 pick.1
  65.1 12.4 %all_to_all.17.got_ref = f32[8,16,128]{2,1,0:T(8,128)S(1)} all-to-all(f32[8,16,128]{2,1,0:T(8,128)S(1)} %pick.1), channel_id=1, replica_groups=mesh['shard'=64,'tp'=8] {'tp'}, dimensions={0} | all-to-all | bytes 131072 | tf_op jit(solution)/shard_map/all_to_all | solution.py:239
  77.5 0.7 finish.1
Async XLA Ops:
  0.0 41.9 %copy-start = (bf16[8,128,512]{2,1,0:T(8,128)(2,1)S(1)}, bf16[8,128,512]{2,1,0:T(8,128)(2,1)}, u32[]{:S(2)}) copy-start(bf16[8,128,512]{2,1,0:T(8,128)(2,1)} %param.13) | copy-start | bytes 3145732

commit v4 on v3

--- a/solution.py
+++ b/solution.py
@@ -6,11 +6,13 @@
 from jax import lax
 from jax.experimental import pallas as pl
 from jax.experimental.pallas import tpu as pltpu
+from jax.sharding import Mesh
 from jax.sharding import PartitionSpec as P
 
 MOST = 4
 LANES = 128
 GROUP = 8
+XS = 4
 VMEM = pl.BlockSpec(memory_space=pltpu.VMEM)
 SMEM = pl.BlockSpec(memory_space=pltpu.SMEM)
 HBM = pl.BlockSpec(memory_space=pltpu.HBM)
@@ -21,7 +23,7 @@
 def pool_kernel(
     local_slots, owners, lens_hbm, probes_hbm, slot_hbm, size_hbm, hid_hbm, lat_hbm,
     pay_ref, ss_ref, route_ref,
-    halves, count, code, lens_ref, probes_ref, slot_ref, size_ref, hid_ref, lat_ref, sems,
+    halves, count, lens_ref, probes_ref, slot_ref, size_ref, hid_ref, lat_ref, sems,
 ):
     tokens, width = hid_ref.shape
     requests, nprobe = probes_ref.shape
@@ -45,12 +47,12 @@
         copy.start()
     for owner in range(owners):
         count[owner] = 0
-        code[owner] = 0
-    pay_ref[...] = jnp.zeros_like(pay_ref)
     for copy in copies:
         copy.wait()
 
-    places = []
+    lane = lax.broadcasted_iota(jnp.int32, (2, LANES), 1)
+    first = lax.broadcasted_iota(jnp.int32, (2, LANES), 0) == 0
+    marks = jnp.full((2, LANES), -1, jnp.int32)
     for query in range(requests):
         for j in range(nprobe):
             item = query * nprobe + j
@@ -59,16 +61,12 @@
             owner = lax.shift_right_logical(slot, bits)
             rank = jnp.minimum(count[owner], MOST - 1)
             count[owner] = rank + 1
-            code[owner] = code[owner] | ((slot & (local_slots - 1)) << (bits * rank))
-            route_ref[0, item] = owner * MOST + rank
+            place = owner * MOST + rank
+            route_ref[0, item] = place
             route_ref[1, item] = size_ref[cluster]
-            places.append((query, owner, rank))
-    side = lax.broadcasted_iota(jnp.int32, (2, LANES), 0)
-    half = bits * MOST // 2
-    for _, owner, _ in places:
-        both = code[owner]
-        mark = jnp.where(side == 0, both & ((1 << half) - 1), lax.shift_right_logical(both, half))
-        pay_ref[owner, MOST * pairs] = mark.astype(jnp.float32).astype(jnp.bfloat16)
+            code = (query << bits) + (slot & (local_slots - 1))
+            marks = jnp.where(lane == item, jnp.where(first, place, code), marks)
+    marks = marks.astype(jnp.float32).astype(jnp.bfloat16)
 
     row_id = lax.broadcasted_iota(jnp.int32, (GROUP, tokens), 0)
     position = lax.broadcasted_iota(jnp.int32, (GROUP, tokens), 1)
@@ -104,29 +102,42 @@
             halves[query * pairs + f // 2, f % 2 : f % 2 + 1, :] = pooled[
                 query : query + 1, f * LANES : (f + 1) * LANES
             ]
-    row = [halves[q * pairs : (q + 1) * pairs].astype(jnp.bfloat16) for q in range(requests)]
-    for query, owner, rank in places:
-        pay_ref[owner, pl.ds(rank * pairs, pairs)] = row[query]
-
-
-def score_kernel(local_slots, owners, rows_ref, pas_ref, out_ref, rows):
+    rows = halves[...].astype(jnp.bfloat16)
+    for place in range(pay_ref.shape[0]):
+        pay_ref[place, : requests * pairs] = rows
+        pay_ref[place, requests * pairs] = marks
+
+
+def score_kernel(local_slots, owners, requests, rows_ref, pas_ref, out_ref, rows):
     cap = out_ref.shape[1]
     pieces = pas_ref.shape[1] // LANES
     block = rows_ref.shape[0] // owners
     bits = local_slots.bit_length() - 1
+    me = (lax.axis_index(("x", "z")) * MOST).astype(jnp.float32)
     rows[...] = rows_ref[...].astype(jnp.float32)
-    query = []
-    local = []
+    place = rows[pl.ds(requests * pieces, owners, stride=block), :]
+    code = rows[pl.ds(requests * pieces + 1, owners, stride=block), :]
+    mine = jnp.concatenate([jnp.where(place == me + float(k), code, 0.0) for k in range(MOST)], axis=0)
+    ones = jnp.ones((LANES, LANES), jnp.bfloat16)
+    code = jnp.dot(mine.astype(jnp.bfloat16), ones, preferred_element_type=jnp.float32).astype(jnp.int32)
+    pieces_of = [
+        [rows[pl.ds(q * pieces + f, owners, stride=block), :] for f in range(pieces)] for q in range(requests)
+    ]
+    chosen = []
     for k in range(MOST):
-        piece = [rows[pl.ds(k * pieces + f, owners, stride=block), :] for f in range(pieces)]
-        query.append(jnp.concatenate(piece, axis=1))
-        mark = rows[pl.ds(MOST * pieces + k // 2, owners, stride=block), :].astype(jnp.int32)
-        local.append(lax.shift_right_logical(mark, bits * (k % 2)) & (local_slots - 1))
-    query = jnp.concatenate(query, axis=0).astype(jnp.bfloat16)
-    local = jnp.concatenate(local, axis=0)
+        query = lax.shift_right_logical(code[k * owners : (k + 1) * owners], bits)
+        piece = []
+        for f in range(pieces):
+            got = pieces_of[0][f]
+            for q in range(1, requests):
+                got = jnp.where(query == q, pieces_of[q][f], got)
+            piece.append(got)
+        chosen.append(jnp.concatenate(piece, axis=1))
+    chosen = jnp.concatenate(chosen, axis=0).astype(jnp.bfloat16)
+    local = code & (local_slots - 1)
     total = jnp.zeros(out_ref.shape, jnp.float32)
     for s in range(local_slots):
-        got = lax.dot_general(query, pas_ref[s * cap : (s + 1) * cap, :], NT, preferred_element_type=jnp.float32)
+        got = lax.dot_general(chosen, pas_ref[s * cap : (s + 1) * cap, :], NT, preferred_element_type=jnp.float32)
         total = total + jnp.where(local == s, got, 0.0)
     for k in range(MOST):
         out_ref[pl.ds(k, owners, stride=MOST), :] = total[k * owners : (k + 1) * owners]
@@ -158,14 +169,14 @@
     out_ref[...] = score.reshape(out_ref.shape)
 
 
-def pool(local_slots, owners, lengths, probes, cluster_slot, slab_sizes, hidden, latents):
+def pool(local_slots, owners, copies, lengths, probes, cluster_slot, slab_sizes, hidden, latents):
     pairs = hidden.shape[1] // LANES // 2
     whole = jnp.int32
     operands = (lengths, probes, cluster_slot, slab_sizes, hidden, latents)
     return pl.pallas_call(
         functools.partial(pool_kernel, local_slots, owners),
         out_shape=(
-            jax.ShapeDtypeStruct((owners, MOST * pairs + 1, 2, LANES), jnp.bfloat16),
+            jax.ShapeDtypeStruct((copies, probes.shape[0] * pairs + 1, 2, LANES), jnp.bfloat16),
             jax.ShapeDtypeStruct((GROUP, LANES), jnp.float32),
             jax.ShapeDtypeStruct((2, probes.size), whole),
         ),
@@ -173,7 +184,6 @@
         out_specs=(VMEM, VMEM, SMEM),
         scratch_shapes=[
             pltpu.VMEM((probes.shape[0] * pairs, 2, LANES), jnp.float32),
-            pltpu.SMEM((owners,), whole),
             pltpu.SMEM((owners,), whole),
             pltpu.SMEM(lengths.shape, whole),
             pltpu.SMEM(probes.shape, whole),
@@ -188,10 +198,10 @@
     )(*(pltpu.with_memory_space_constraint(x, pltpu.HBM) for x in operands))
 
 
-def score(owners, rows, passages):
+def score(owners, requests, rows, passages):
     local_slots, cap, width = passages.shape
     return pl.pallas_call(
-        functools.partial(score_kernel, local_slots, owners),
+        functools.partial(score_kernel, local_slots, owners, requests),
         out_shape=jax.ShapeDtypeStruct((owners * MOST, cap), jnp.float32),
         in_specs=[VMEM, VMEM],
         out_specs=VMEM,
@@ -226,34 +236,41 @@
     )(parts)
 
 
-def per_device(shards, tps, hidden, latents, lengths, probes, cluster_slot, slab_sizes, passages):
+def per_device(xs, zs, tps, hidden, latents, lengths, probes, cluster_slot, slab_sizes, passages):
+    shards = xs * zs
     local_slots, cap, _ = passages.shape
     requests, nprobe = probes.shape
     payload, squares, route = pool(
-        local_slots, shards, lengths, probes, cluster_slot, slab_sizes, hidden, latents
+        local_slots, shards, zs, lengths, probes, cluster_slot, slab_sizes, hidden, latents
     )
-    rows = lax.all_to_all(payload, "shard", 0, 0, tiled=True)
-    scores = score(shards, rows.reshape(-1, LANES), passages)
-    got = lax.all_to_all(scores.reshape(shards, 1, MOST * cap), "shard", 0, 0, tiled=True)
+    blocks = lax.all_to_all(payload, "z", 0, 0, tiled=True)
+    blocks = jnp.broadcast_to(blocks[None], (xs, *blocks.shape))
+    rows = lax.all_to_all(blocks, "x", 0, 0, tiled=True)
+    scores = score(shards, requests, rows.reshape(-1, LANES), passages)
+    got = lax.all_to_all(scores.reshape(shards, 1, MOST * cap), ("x", "z"), 0, 0, tiled=True)
     picked = pick(tps, requests, route, got.reshape(scores.shape), squares)
     parts = lax.all_to_all(picked, "tp", 0, 0, tiled=True)
     return finish(requests, nprobe, parts)
 
 
 def solution(mesh):
+    tps = mesh.shape["tp"]
+    zs = mesh.shape["shard"] // XS
+    fine = Mesh(mesh.devices.reshape(XS, zs, tps), ("x", "z", "tp"))
+    shard = ("x", "z")
     placed = (
-        P("shard", "tp"),
+        P(shard, "tp"),
         P(None, "tp"),
-        P("shard", None),
-        P("shard", None),
+        P(shard, None),
+        P(shard, None),
         P(),
         P(),
-        P("shard", None, "tp"),
+        P(shard, None, "tp"),
     )
     return jax.shard_map(
-        functools.partial(per_device, mesh.shape["shard"], mesh.shape["tp"]),
-        mesh=mesh,
+        functools.partial(per_device, XS, zs, tps),
+        mesh=fine,
         in_specs=placed,
-        out_specs=P("shard", None, "tp"),
+        out_specs=P(shard, None, "tp"),
         check_vma=False,
     )

time: 78.4 us -> 74.6 us (0.952)
  blocking collectives: 73.1 us -> 69.2 us
    all_to_all x2 -> x3, blocking collectives: 60.7 us -> 56.2 us  [the longest x1 27.2 us: per_device(): blocks = lax.all_to_all(payload, 'z', 0, 0, tiled=True)]
where the time goes in v4:
time: 74.6 us; the launch traced here: 74.3 us
  blocking collectives  69.2 us (93%)
  Pallas kernels  4.99 us (7%)
    all_to_all x1, blocking collectives, per_device(): blocks = lax.all_to_all(payload, 'z', 0, 0, tiled=True)  27.2 us
    all_to_all x1, blocking collectives, per_device(): lax.all_to_all(scores.reshape(shards, 1, MOST * cap), ('x', 'z'), 0, 0, t...  19.5 us
    all_to_all x1, blocking collectives, per_device(): parts = lax.all_to_all(picked, 'tp', 0, 0, tiled=True)  12.9 us
    all_to_all x1, blocking collectives, per_device(): rows = lax.all_to_all(blocks, 'x', 0, 0, tiled=True)  9.52 us
    pallas_call x1, Pallas kernels, pool(): pl.pallas_call(functools.partial(pool_kernel, local_slots, owners), out_s...  2.67 us

profile of v4, /device:TPU:1, one launch (start us, length us, event | category | flops | bytes accessed | tf_op | source)
XLA Modules:
  0.0 74.3 jit_solution(2406854381434524183)
XLA Ops:
  0.0 0.0 copy-start
  0.0 2.7 %pool.1 = (bf16[16,9,2,128]{3,2,1,0:T(2,128)(2,1)S(1)}, f32[8,128]{1,0:T(8,128)S(1)}, s32[2,32]{1,0:T(2,128)S(1)}) custom-call(s32[1,4]{1,0:T(1,128)} %lens_hbm.1, s32[4,8]{1,0:T(4,128)} %probes_hbm.1, s32[512]{0:T(512)} %slot_hbm.1, s32[512]{0:T(512)} %size_hbm.1, bf16[512,512]{1,0:T(8,128)(2,1)} %hid_hbm.1, bf16[512,512]{1,0:T(8,128)(2,1)} %lat_hbm.1), custom_call_target="tpu_custom_call" | custom-call | tf_op jit(solution)/shard_map/pool/pallas_call | solution.py:176
  2.7 27.2 %all_to_all.20 = bf16[16,9,2,128]{3,2,1,0:T(2,128)(2,1)S(1)} all-to-all(bf16[16,9,2,128]{3,2,1,0:T(2,128)(2,1)S(1)} %get-tuple-element.9), channel_id=1, replica_groups=mesh['x'=4,'z'=16,'tp'=8] {'z'}, dimensions={0} | all-to-all | bytes 147456 | tf_op jit(solution)/shard_map/all_to_all | solution.py:246
  29.9 0.2 broadcast_in_dim.2
  30.1 9.5 %all_to_all.21 = bf16[4,16,9,2,128]{4,3,2,1,0:T(2,128)(2,1)S(1)} all-to-all(bf16[4,16,9,2,128]{4,3,2,1,0:T(2,128)(2,1)S(1)} %broadcast_in_dim.2), channel_id=1, replica_groups=mesh['x'=4,'z'=16,'tp'=8] {'x'}, dimensions={0} | all-to-all | bytes 589824 | tf_op jit(solution)/shard_map/all_to_all | solution.py:248
  39.6 0.0 copy-done
  39.6 0.9 %score.1 = f32[256,128]{1,0:T(8,128)S(1)} custom-call(bf16[1152,128]{1,0:T(8,128)(2,1)S(1)} %bitcast.4, bf16[1024,512]{1,0:T(8,128)(2,1)S(1)} %bitcast.5), custom_call_target="tpu_custom_call" | custom-call | tf_op jit(solution)/shard_map/score/pallas_call | solution.py:203
  40.6 19.5 %all_to_all.22 = f32[64,1,512]{2,1,0:T(1,128)S(1)} all-to-all(f32[64,1,512]{2,1,0:T(1,128)S(1)} %bitcast.6), channel_id=1, replica_groups=mesh['x'=4,'z'=16,'tp'=8] {'x','z'}, dimensions={0} | all-to-all | bytes 262144 | tf_op jit(solution)/shard_map/all_to_all | solution.py:250
  60.0 0.7 pick.1
  60.7 12.9 %all_to_all.23.got_ref = f32[8,16,128]{2,1,0:T(8,128)S(1)} all-to-all(f32[8,16,128]{2,1,0:T(8,128)S(1)} %pick.1), channel_id=1, replica_groups=mesh['x'=4,'z'=16,'tp'=8] {'tp'}, dimensions={0} | all-to-all | bytes 131072 | tf_op jit(solution)/shard_map/all_to_all | solution.py:252
  73.6 0.7 finish.1
Async XLA Ops:
  0.0 39.6 %copy-start = (bf16[8,128,512]{2,1,0:T(8,128)(2,1)S(1)}, bf16[8,128,512]{2,1,0:T(8,128)(2,1)}, u32[]{:S(2)}) copy-start(bf16[8,128,512]{2,1,0:T(8,128)(2,1)} %param.13) | copy-start | bytes 3145732

commit v5 on v4

--- a/solution.py
+++ b/solution.py
@@ -21,7 +21,7 @@
 
 
 def pool_kernel(
-    local_slots, owners, lens_hbm, probes_hbm, slot_hbm, size_hbm, hid_hbm, lat_hbm,
+    local_slots, xs, zs, lens_hbm, probes_hbm, slot_hbm, size_hbm, hid_hbm, lat_hbm,
     pay_ref, ss_ref, route_ref,
     halves, count, lens_ref, probes_ref, slot_ref, size_ref, hid_ref, lat_ref, sems,
 ):
@@ -45,7 +45,7 @@
     ]
     for copy in copies:
         copy.start()
-    for owner in range(owners):
+    for owner in range(xs * zs):
         count[owner] = 0
     for copy in copies:
         copy.wait()
@@ -62,7 +62,9 @@
             rank = jnp.minimum(count[owner], MOST - 1)
             count[owner] = rank + 1
             place = owner * MOST + rank
-            route_ref[0, item] = place
+            x, z = lax.shift_right_logical(owner, zs.bit_length() - 1), owner & (zs - 1)
+            group = (x & 1) * MOST + rank
+            route_ref[0, item] = group * (zs * xs // 2) + z * (xs // 2) + lax.shift_right_logical(x, 1)
             route_ref[1, item] = size_ref[cluster]
             code = (query << bits) + (slot & (local_slots - 1))
             marks = jnp.where(lane == item, jnp.where(first, place, code), marks)
@@ -108,8 +110,9 @@
         pay_ref[place, requests * pairs] = marks
 
 
-def score_kernel(local_slots, owners, requests, rows_ref, pas_ref, out_ref, rows):
-    cap = out_ref.shape[1]
+def score_kernel(local_slots, xs, zs, requests, rows_ref, pas_ref, ss_ref, out_ref, rows, blocks):
+    owners = xs * zs
+    cap = LANES
     pieces = pas_ref.shape[1] // LANES
     block = rows_ref.shape[0] // owners
     bits = local_slots.bit_length() - 1
@@ -135,48 +138,88 @@
         chosen.append(jnp.concatenate(piece, axis=1))
     chosen = jnp.concatenate(chosen, axis=0).astype(jnp.bfloat16)
     local = code & (local_slots - 1)
-    total = jnp.zeros(out_ref.shape, jnp.float32)
+    total = jnp.zeros((MOST * owners, cap), jnp.float32)
     for s in range(local_slots):
         got = lax.dot_general(chosen, pas_ref[s * cap : (s + 1) * cap, :], NT, preferred_element_type=jnp.float32)
         total = total + jnp.where(local == s, got, 0.0)
-    for k in range(MOST):
-        out_ref[pl.ds(k, owners, stride=MOST), :] = total[k * owners : (k + 1) * owners]
-
-
-def pick_kernel(requests, route_ref, got_ref, ss_ref, out_ref, buf):
-    items = route_ref.shape[1]
-    nprobe = items // requests
+
+    tps = zs // GROUP * MOST
+    part = LANES // tps
+    height = out_ref.shape[0] // (xs * tps)
+    lane = lax.broadcasted_iota(jnp.int32, (GROUP, LANES), 1)
+    for x in range(xs):
+        first = [k * owners + x * zs + h * GROUP for h in range(zs // GROUP) for k in range(MOST)]
+        skew = [total[r : r + GROUP] for r in first]
+        skew = [pltpu.roll(v, part * g, 1) if g else v for g, v in enumerate(skew)]
+        for t in range(tps):
+            mixed = skew[0]
+            for g in range(1, tps):
+                mixed = jnp.where(lane // part == (t + g) % tps, skew[g], mixed)
+            mixed = pltpu.roll(mixed, LANES - part * t, 1) if t else mixed
+            row = (x * tps + t) * height
+            blocks[row : row + GROUP, :] = mixed
     lane = lax.broadcasted_iota(jnp.int32, (1, LANES), 1)
-    buf[2 * items :, :] = jnp.zeros((LANES - 2 * items, buf.shape[1]), jnp.float32)
-    for item in range(items):
-        row = got_ref[pl.ds(route_ref[0, item], 1), :]
-        buf[item : item + 1, :] = jnp.where(lane < route_ref[1, item], row, 0.0)
-    for query in range(requests):
-        first = items + query * nprobe
-        buf[first : first + nprobe, :] = jnp.broadcast_to(ss_ref[query : query + 1, :], (nprobe, LANES))
-    out_ref[...] = buf[...].T.reshape(out_ref.shape)
-
-
-def finish_kernel(items, got_ref, out_ref, buf):
-    cap = got_ref.shape[1]
-    buf[cap:, :] = jnp.zeros((LANES - cap, LANES), jnp.float32)
-    total = got_ref[0]
-    for t in range(1, got_ref.shape[0]):
-        total = total + got_ref[t]
-    buf[:cap, :] = total
-    turned = buf[...].T
-    score = turned[:items, :cap] / jnp.sqrt(turned[items : 2 * items, :cap] + 1e-06)
-    out_ref[...] = score.reshape(out_ref.shape)
-
-
-def pool(local_slots, owners, copies, lengths, probes, cluster_slot, slab_sizes, hidden, latents):
+    squares = ss_ref[0:1, :]
+    for q in range(1, requests):
+        squares = jnp.where(lane % (LANES // 2) // part == q, ss_ref[q : q + 1, :], squares)
+    hi = squares.astype(jnp.bfloat16).astype(jnp.float32)
+    mid = (squares - hi).astype(jnp.bfloat16).astype(jnp.float32)
+    parts = jnp.concatenate([jnp.where(lane < LANES // 2, hi, mid), squares - hi - mid], axis=0)
+    for i in range(xs * tps):
+        blocks[i * height + GROUP : (i + 1) * height, :] = parts
+    out_ref[...] = blocks[...].astype(jnp.bfloat16)
+
+
+def merge_kernel(xs, tps, got_ref, out_ref, ss_ref, blocks):
+    height = blocks.shape[0] // (xs * tps)
+    blocks[...] = got_ref[...].astype(jnp.float32)
+    total = []
+    for x in range(xs):
+        acc = blocks[x * tps * height : x * tps * height + GROUP, :]
+        for t in range(1, tps):
+            row = (x * tps + t) * height
+            acc = acc + blocks[row : row + GROUP, :]
+        total.append(acc)
+    left = lax.broadcasted_iota(jnp.int32, (GROUP, LANES), 1) < LANES // 2
+    halves = xs // 2
+    for r in range(halves):
+        one, two = total[2 * r], total[2 * r + 1]
+        near = jnp.where(left, one, pltpu.roll(two, LANES // 2, 1))
+        far = jnp.where(left, pltpu.roll(one, LANES // 2, 1), two)
+        out_ref[pl.ds(r, GROUP, stride=halves), :] = near
+        out_ref[pl.ds(GROUP * halves + r, GROUP, stride=halves), :] = far
+    mine = lax.axis_index("x") * (tps * height) + GROUP
+    top = blocks[pl.ds(mine, 1), :]
+    low = blocks[pl.ds(mine + 1, 1), :]
+    for t in range(1, tps):
+        top = top + blocks[pl.ds(mine + t * height, 1), :]
+        low = low + blocks[pl.ds(mine + t * height + 1, 1), :]
+    ss_ref[...] = jnp.broadcast_to(top + pltpu.roll(top, LANES // 2, 1) + low, ss_ref.shape)
+
+
+def finish_kernel(route_ref, got_ref, ss_ref, out_ref, turned, buf):
+    requests, nprobe, part = out_ref.shape
+    height = got_ref.shape[0]
+    for g in range(LANES // part):
+        turned[g * height : (g + 1) * height, :] = pltpu.roll(got_ref[...], LANES - part * g, 1) if g else got_ref[...]
+    column = lax.broadcasted_iota(jnp.int32, (1, LANES), 1) + lax.axis_index("tp") * part
+    for item in range(requests * nprobe):
+        row = turned[pl.ds(route_ref[0, item], 1), :]
+        buf[item : item + 1, :] = jnp.where(column < route_ref[1, item], row, 0.0)
+    norm = jnp.sqrt(ss_ref[...] + 1e-06)
+    for q in range(requests):
+        here = pltpu.roll(norm, LANES - part * q, 1) if q else norm
+        out_ref[q] = (buf[q * nprobe : (q + 1) * nprobe, :] / here)[:, :part]
+
+
+def pool(local_slots, xs, zs, lengths, probes, cluster_slot, slab_sizes, hidden, latents):
     pairs = hidden.shape[1] // LANES // 2
     whole = jnp.int32
     operands = (lengths, probes, cluster_slot, slab_sizes, hidden, latents)
     return pl.pallas_call(
-        functools.partial(pool_kernel, local_slots, owners),
+        functools.partial(pool_kernel, local_slots, xs, zs),
         out_shape=(
-            jax.ShapeDtypeStruct((copies, probes.shape[0] * pairs + 1, 2, LANES), jnp.bfloat16),
+            jax.ShapeDtypeStruct((zs, probes.shape[0] * pairs + 1, 2, LANES), jnp.bfloat16),
             jax.ShapeDtypeStruct((GROUP, LANES), jnp.float32),
             jax.ShapeDtypeStruct((2, probes.size), whole),
         ),
@@ -184,7 +227,7 @@
         out_specs=(VMEM, VMEM, SMEM),
         scratch_shapes=[
             pltpu.VMEM((probes.shape[0] * pairs, 2, LANES), jnp.float32),
-            pltpu.SMEM((owners,), whole),
+            pltpu.SMEM((xs * zs,), whole),
             pltpu.SMEM(lengths.shape, whole),
             pltpu.SMEM(probes.shape, whole),
             pltpu.SMEM(cluster_slot.shape, whole),
@@ -198,59 +241,64 @@
     )(*(pltpu.with_memory_space_constraint(x, pltpu.HBM) for x in operands))
 
 
-def score(owners, requests, rows, passages):
+def score(xs, zs, tps, requests, rows, passages, squares):
     local_slots, cap, width = passages.shape
+    blocks = (xs * tps * (GROUP + 2), LANES)
     return pl.pallas_call(
-        functools.partial(score_kernel, local_slots, owners, requests),
-        out_shape=jax.ShapeDtypeStruct((owners * MOST, cap), jnp.float32),
-        in_specs=[VMEM, VMEM],
+        functools.partial(score_kernel, local_slots, xs, zs, requests),
+        out_shape=jax.ShapeDtypeStruct(blocks, jnp.bfloat16),
+        in_specs=[VMEM, VMEM, VMEM],
         out_specs=VMEM,
-        scratch_shapes=[pltpu.VMEM(rows.shape, jnp.float32)],
+        scratch_shapes=[pltpu.VMEM(rows.shape, jnp.float32), pltpu.VMEM(blocks, jnp.float32)],
         name="score",
         compiler_params=PARAMS,
-    )(rows, passages.reshape(local_slots * cap, width))
-
-
-def pick(tps, requests, route, got, squares):
-    cap = got.shape[1]
+    )(rows, passages.reshape(local_slots * cap, width), squares)
+
+
+def merge(xs, zs, tps, got):
     return pl.pallas_call(
-        functools.partial(pick_kernel, requests),
-        out_shape=jax.ShapeDtypeStruct((tps, cap // tps, LANES), jnp.float32),
+        functools.partial(merge_kernel, xs, tps),
+        out_shape=(
+            jax.ShapeDtypeStruct((zs * xs // 2, LANES), jnp.float32),
+            jax.ShapeDtypeStruct((GROUP, LANES), jnp.float32),
+        ),
+        in_specs=[VMEM],
+        out_specs=(VMEM, VMEM),
+        scratch_shapes=[pltpu.VMEM(got.shape, jnp.float32)],
+        name="merge",
+        compiler_params=PARAMS,
+    )(got)
+
+
+def finish(requests, nprobe, part, route, got, squares):
+    return pl.pallas_call(
+        finish_kernel,
+        out_shape=jax.ShapeDtypeStruct((requests, nprobe, part), jnp.float32),
         in_specs=[SMEM, VMEM, VMEM],
         out_specs=VMEM,
-        scratch_shapes=[pltpu.VMEM((LANES, cap), jnp.float32)],
-        name="pick",
+        scratch_shapes=[
+            pltpu.VMEM((LANES // part * got.shape[0], LANES), jnp.float32),
+            pltpu.VMEM((requests * nprobe, LANES), jnp.float32),
+        ],
+        name="finish",
         compiler_params=PARAMS,
     )(route, got, squares)
 
 
-def finish(requests, nprobe, parts):
-    return pl.pallas_call(
-        functools.partial(finish_kernel, requests * nprobe),
-        out_shape=jax.ShapeDtypeStruct((requests, nprobe, parts.shape[1]), jnp.float32),
-        in_specs=[VMEM],
-        out_specs=VMEM,
-        scratch_shapes=[pltpu.VMEM((LANES, LANES), jnp.float32)],
-        name="finish",
-        compiler_params=PARAMS,
-    )(parts)
-
-
 def per_device(xs, zs, tps, hidden, latents, lengths, probes, cluster_slot, slab_sizes, passages):
-    shards = xs * zs
     local_slots, cap, _ = passages.shape
     requests, nprobe = probes.shape
     payload, squares, route = pool(
-        local_slots, shards, zs, lengths, probes, cluster_slot, slab_sizes, hidden, latents
+        local_slots, xs, zs, lengths, probes, cluster_slot, slab_sizes, hidden, latents
     )
     blocks = lax.all_to_all(payload, "z", 0, 0, tiled=True)
     blocks = jnp.broadcast_to(blocks[None], (xs, *blocks.shape))
-    rows = lax.all_to_all(blocks, "x", 0, 0, tiled=True)
-    scores = score(shards, requests, rows.reshape(-1, LANES), passages)
-    got = lax.all_to_all(scores.reshape(shards, 1, MOST * cap), ("x", "z"), 0, 0, tiled=True)
-    picked = pick(tps, requests, route, got.reshape(scores.shape), squares)
-    parts = lax.all_to_all(picked, "tp", 0, 0, tiled=True)
-    return finish(requests, nprobe, parts)
+    rows = lax.all_to_all(blocks, "x", 0, 0, tiled=True).reshape(-1, LANES)
+    partial = score(xs, zs, tps, requests, rows, passages, squares)
+    blocks = lax.all_to_all(partial.reshape(xs * tps, -1, 2, LANES), ("x", "tp"), 0, 0, tiled=True)
+    columns, squares = merge(xs, zs, tps, blocks.reshape(partial.shape))
+    got = lax.all_to_all(columns.reshape(zs, 1, -1), "z", 0, 0, tiled=True)
+    return finish(requests, nprobe, cap // tps, route, got.reshape(columns.shape), squares)
 
 
 def solution(mesh):

time: 74.6 us -> 72.5 us (0.972)
  blocking collectives: 69.2 us -> 66.9 us
    all_to_all x3, blocking collectives: 41.9 us -> 39.6 us  [the longest x1 16.2 us: per_device(): lax.all_to_all(partial.reshape(xs * tps, -1, 2, LANES), ('x', 'tp'), 0, 0...]
where the time goes in v5:
time: 72.5 us; the launch traced here: 72.2 us
  blocking collectives  66.9 us (92%)
  Pallas kernels  5.18 us (7%)
    all_to_all x1, blocking collectives, per_device(): blocks = lax.all_to_all(payload, 'z', 0, 0, tiled=True)  27.2 us
    all_to_all x1, blocking collectives, per_device(): lax.all_to_all(partial.reshape(xs * tps, -1, 2, LANES), ('x', 'tp'), 0, 0...  16.2 us
    all_to_all x1, blocking collectives, per_device(): got = lax.all_to_all(columns.reshape(zs, 1, -1), 'z', 0, 0, tiled=True)  13.9 us
    all_to_all x1, blocking collectives, per_device(): rows = lax.all_to_all(blocks, 'x', 0, 0, tiled=True).reshape(-1, LANES)  9.52 us
    pallas_call x1, Pallas kernels, pool(): pl.pallas_call(functools.partial(pool_kernel, local_slots, xs, zs), out_s...  2.7 us

profile of v5, /device:TPU:1, one launch (start us, length us, event | category | flops | bytes accessed | tf_op | source)
XLA Modules:
  0.0 72.2 jit_solution(7557280518875350239)
XLA Ops:
  0.0 0.0 copy-start
  0.0 2.7 %pool.1 = (bf16[16,9,2,128]{3,2,1,0:T(2,128)(2,1)S(1)}, f32[8,128]{1,0:T(8,128)S(1)}, s32[2,32]{1,0:T(2,128)S(1)}) custom-call(s32[1,4]{1,0:T(1,128)} %lens_hbm.1, s32[4,8]{1,0:T(4,128)} %probes_hbm.1, s32[512]{0:T(512)} %slot_hbm.1, s32[512]{0:T(512)} %size_hbm.1, bf16[512,512]{1,0:T(8,128)(2,1)} %hid_hbm.1, bf16[512,512]{1,0:T(8,128)(2,1)} %lat_hbm.1), custom_call_target="tpu_custom_call" | custom-call | tf_op jit(solution)/shard_map/pool/pallas_call | solution.py:219
  2.7 27.2 %all_to_all.20 = bf16[16,9,2,128]{3,2,1,0:T(2,128)(2,1)S(1)} all-to-all(bf16[16,9,2,128]{3,2,1,0:T(2,128)(2,1)S(1)} %get-tuple-element.11), channel_id=1, replica_groups=mesh['x'=4,'z'=16,'tp'=8] {'z'}, dimensions={0} | all-to-all | bytes 147456 | tf_op jit(solution)/shard_map/all_to_all | solution.py:294
  30.0 0.2 broadcast_in_dim.2
  30.1 9.5 %all_to_all.21 = bf16[4,16,9,2,128]{4,3,2,1,0:T(2,128)(2,1)S(1)} all-to-all(bf16[4,16,9,2,128]{4,3,2,1,0:T(2,128)(2,1)S(1)} %broadcast_in_dim.2), channel_id=1, replica_groups=mesh['x'=4,'z'=16,'tp'=8] {'x'}, dimensions={0} | all-to-all | bytes 589824 | tf_op jit(solution)/shard_map/all_to_all | solution.py:296
  39.6 0.0 copy-done
  39.6 1.1 %score.1 = bf16[320,128]{1,0:T(8,128)(2,1)S(1)} custom-call(bf16[1152,128]{1,0:T(8,128)(2,1)S(1)} %bitcast.6, bf16[1024,512]{1,0:T(8,128)(2,1)S(1)} %bitcast.7, f32[8,128]{1,0:T(8,128)S(1)} %get-tuple-element.12.ss_ref), custom_call_target="tpu_custom_call" | custom-call | tf_op jit(solution)/shard_map/score/pallas_call | solution.py:247
  40.7 16.2 %all_to_all.22 = bf16[32,5,2,128]{3,2,1,0:T(2,128)(2,1)S(1)} all-to-all(bf16[32,5,2,128]{3,2,1,0:T(2,128)(2,1)S(1)} %bitcast.8), channel_id=1, replica_groups=mesh['x'=4,'z'=16,'tp'=8] {'x','tp'}, dimensions={0} | all-to-all | bytes 163840 | tf_op jit(solution)/shard_map/all_to_all | solution.py:298
  56.9 0.1 merge.1
  57.0 13.9 %all_to_all.23 = f32[16,1,256]{2,1,0:T(1,128)S(1)} all-to-all(f32[16,1,256]{2,1,0:T(1,128)S(1)} %bitcast.11), channel_id=1, replica_groups=mesh['x'=4,'z'=16,'tp'=8] {'z'}, dimensions={0} | all-to-all | bytes 32768 | tf_op jit(solution)/shard_map/all_to_all | solution.py:300
  70.9 1.3 %finish.1 = f32[4,8,16]{2,1,0:T(8,128)} custom-call(s32[2,32]{1,0:T(2,128)S(1)} %get-tuple-element.10.route_ref, f32[32,128]{1,0:T(8,128)S(1)} %bitcast.10, f32[8,128]{1,0:T(8,128)S(1)} %get-tuple-element.14.ss_ref), custom_call_target="tpu_custom_call" | custom-call | tf_op jit(solution)/shard_map/finish/pallas_call | solution.py:274
Async XLA Ops:
  0.0 39.6 %copy-start = (bf16[8,128,512]{2,1,0:T(8,128)(2,1)S(1)}, bf16[8,128,512]{2,1,0:T(8,128)(2,1)}, u32[]{:S(2)}) copy-start(bf16[8,128,512]{2,1,0:T(8,128)(2,1)} %param.13) | copy-start | bytes 3145732

commit v6 on v5

--- a/solution.py
+++ b/solution.py
@@ -14,15 +14,21 @@
 GROUP = 8
 XS = 4
 VMEM = pl.BlockSpec(memory_space=pltpu.VMEM)
-SMEM = pl.BlockSpec(memory_space=pltpu.SMEM)
 HBM = pl.BlockSpec(memory_space=pltpu.HBM)
 NT = (((1,), (1,)), ((), ()))
 PARAMS = pltpu.CompilerParams(vmem_limit_bytes=16 << 20)
 
 
+def three_parts(value):
+    hi = value.astype(jnp.bfloat16).astype(jnp.float32)
+    rest = value - hi
+    mid = rest.astype(jnp.bfloat16).astype(jnp.float32)
+    return hi, mid, rest - mid
+
+
 def pool_kernel(
-    local_slots, xs, zs, lens_hbm, probes_hbm, slot_hbm, size_hbm, hid_hbm, lat_hbm,
-    pay_ref, ss_ref, route_ref,
+    local_slots, xs, zs, tps, lens_hbm, probes_hbm, slot_hbm, size_hbm, hid_hbm, lat_hbm,
+    pay_ref, ss_ref, sel_ref,
     halves, count, lens_ref, probes_ref, slot_ref, size_ref, hid_ref, lat_ref, sems,
 ):
     tokens, width = hid_ref.shape
@@ -47,9 +53,13 @@
         copy.start()
     for owner in range(xs * zs):
         count[owner] = 0
-    for copy in copies:
+    for copy in copies[:4]:
         copy.wait()
 
+    spot = lax.broadcasted_iota(jnp.int32, (1, LANES), 1)
+    part = LANES // tps
+    column = (spot & (part - 1)) + lax.axis_index("tp") * part
+    group_of = lax.shift_right_logical(spot, part.bit_length() - 1)
     lane = lax.broadcasted_iota(jnp.int32, (2, LANES), 1)
     first = lax.broadcasted_iota(jnp.int32, (2, LANES), 0) == 0
     marks = jnp.full((2, LANES), -1, jnp.int32)
@@ -63,12 +73,15 @@
             count[owner] = rank + 1
             place = owner * MOST + rank
             x, z = lax.shift_right_logical(owner, zs.bit_length() - 1), owner & (zs - 1)
-            group = (x & 1) * MOST + rank
-            route_ref[0, item] = group * (zs * xs // 2) + z * (xs // 2) + lax.shift_right_logical(x, 1)
-            route_ref[1, item] = size_ref[cluster]
+            row = z * (xs // 2) + lax.shift_right_logical(x, 1)
+            here = (group_of == (x & 1) * MOST + rank) & (column < size_ref[cluster])
+            sel_ref[item : item + 1, :LANES] = jnp.where(spot == row, 1.0, 0.0)
+            sel_ref[item : item + 1, LANES:] = jnp.where(here, 1.0, 0.0)
             code = (query << bits) + (slot & (local_slots - 1))
             marks = jnp.where(lane == item, jnp.where(first, place, code), marks)
     marks = marks.astype(jnp.float32).astype(jnp.bfloat16)
+    for copy in copies[4:]:
+        copy.wait()
 
     row_id = lax.broadcasted_iota(jnp.int32, (GROUP, tokens), 0)
     position = lax.broadcasted_iota(jnp.int32, (GROUP, tokens), 1)
@@ -90,10 +103,7 @@
     e = jnp.exp2((logits - top) * (math.log2(math.e) / math.sqrt(width)))
     weights = (e * (1.0 / jnp.sum(e, axis=1, keepdims=True))).astype(jnp.bfloat16)
     total = jnp.dot(member, weights, preferred_element_type=jnp.float32)
-    hi = total.astype(jnp.bfloat16).astype(jnp.float32)
-    rest = total - hi
-    mid = rest.astype(jnp.bfloat16).astype(jnp.float32)
-    parts = jnp.concatenate([hi, mid, rest - mid, jnp.zeros_like(hi)], axis=0).astype(jnp.bfloat16)
+    parts = jnp.concatenate([*three_parts(total), jnp.zeros_like(total)], axis=0).astype(jnp.bfloat16)
     sums = jnp.dot(parts, lat, preferred_element_type=jnp.float32)
     sums = sums[:GROUP] + sums[GROUP : 2 * GROUP] + sums[2 * GROUP : 3 * GROUP]
     pooled = sums / length.astype(jnp.float32)
@@ -162,9 +172,8 @@
     squares = ss_ref[0:1, :]
     for q in range(1, requests):
         squares = jnp.where(lane % (LANES // 2) // part == q, ss_ref[q : q + 1, :], squares)
-    hi = squares.astype(jnp.bfloat16).astype(jnp.float32)
-    mid = (squares - hi).astype(jnp.bfloat16).astype(jnp.float32)
-    parts = jnp.concatenate([jnp.where(lane < LANES // 2, hi, mid), squares - hi - mid], axis=0)
+    hi, mid, low = three_parts(squares)
+    parts = jnp.concatenate([jnp.where(lane < LANES // 2, hi, mid), low], axis=0)
     for i in range(xs * tps):
         blocks[i * height + GROUP : (i + 1) * height, :] = parts
     out_ref[...] = blocks[...].astype(jnp.bfloat16)
@@ -197,34 +206,37 @@
     ss_ref[...] = jnp.broadcast_to(top + pltpu.roll(top, LANES // 2, 1) + low, ss_ref.shape)
 
 
-def finish_kernel(route_ref, got_ref, ss_ref, out_ref, turned, buf):
+def finish_kernel(sel_ref, got_ref, ss_ref, out_ref):
     requests, nprobe, part = out_ref.shape
     height = got_ref.shape[0]
-    for g in range(LANES // part):
-        turned[g * height : (g + 1) * height, :] = pltpu.roll(got_ref[...], LANES - part * g, 1) if g else got_ref[...]
-    column = lax.broadcasted_iota(jnp.int32, (1, LANES), 1) + lax.axis_index("tp") * part
-    for item in range(requests * nprobe):
-        row = turned[pl.ds(route_ref[0, item], 1), :]
-        buf[item : item + 1, :] = jnp.where(column < route_ref[1, item], row, 0.0)
+    one_hot = sel_ref[:, :height].astype(jnp.bfloat16)
+    parts = jnp.concatenate(three_parts(got_ref[...]), axis=1).astype(jnp.bfloat16)
+    rows = jnp.dot(one_hot, parts, preferred_element_type=jnp.float32)
+    rows = rows[:, :LANES] + rows[:, LANES : 2 * LANES] + rows[:, 2 * LANES :]
+    rows = jnp.where(sel_ref[:, LANES:] > 0.0, rows, 0.0)
+    step = LANES // 2
+    while step >= part:
+        rows = rows + pltpu.roll(rows, step, 1)
+        step //= 2
     norm = jnp.sqrt(ss_ref[...] + 1e-06)
     for q in range(requests):
         here = pltpu.roll(norm, LANES - part * q, 1) if q else norm
-        out_ref[q] = (buf[q * nprobe : (q + 1) * nprobe, :] / here)[:, :part]
-
-
-def pool(local_slots, xs, zs, lengths, probes, cluster_slot, slab_sizes, hidden, latents):
+        out_ref[q] = (rows[q * nprobe : (q + 1) * nprobe, :] / here)[:, :part]
+
+
+def pool(local_slots, xs, zs, tps, lengths, probes, cluster_slot, slab_sizes, hidden, latents):
     pairs = hidden.shape[1] // LANES // 2
     whole = jnp.int32
     operands = (lengths, probes, cluster_slot, slab_sizes, hidden, latents)
     return pl.pallas_call(
-        functools.partial(pool_kernel, local_slots, xs, zs),
+        functools.partial(pool_kernel, local_slots, xs, zs, tps),
         out_shape=(
             jax.ShapeDtypeStruct((zs, probes.shape[0] * pairs + 1, 2, LANES), jnp.bfloat16),
             jax.ShapeDtypeStruct((GROUP, LANES), jnp.float32),
-            jax.ShapeDtypeStruct((2, probes.size), whole),
+            jax.ShapeDtypeStruct((probes.size, 2 * LANES), jnp.float32),
         ),
         in_specs=[HBM] * len(operands),
-        out_specs=(VMEM, VMEM, SMEM),
+        out_specs=(VMEM, VMEM, VMEM),
         scratch_shapes=[
             pltpu.VMEM((probes.shape[0] * pairs, 2, LANES), jnp.float32),
             pltpu.SMEM((xs * zs,), whole),
@@ -270,26 +282,22 @@
     )(got)
 
 
-def finish(requests, nprobe, part, route, got, squares):
+def finish(requests, nprobe, part, select, got, squares):
     return pl.pallas_call(
         finish_kernel,
         out_shape=jax.ShapeDtypeStruct((requests, nprobe, part), jnp.float32),
-        in_specs=[SMEM, VMEM, VMEM],
+        in_specs=[VMEM, VMEM, VMEM],
         out_specs=VMEM,
-        scratch_shapes=[
-            pltpu.VMEM((LANES // part * got.shape[0], LANES), jnp.float32),
-            pltpu.VMEM((requests * nprobe, LANES), jnp.float32),
-        ],
         name="finish",
         compiler_params=PARAMS,
-    )(route, got, squares)
+    )(select, got, squares)
 
 
 def per_device(xs, zs, tps, hidden, latents, lengths, probes, cluster_slot, slab_sizes, passages):
     local_slots, cap, _ = passages.shape
     requests, nprobe = probes.shape
-    payload, squares, route = pool(
-        local_slots, xs, zs, lengths, probes, cluster_slot, slab_sizes, hidden, latents
+    payload, squares, select = pool(
+        local_slots, xs, zs, tps, lengths, probes, cluster_slot, slab_sizes, hidden, latents
     )
     blocks = lax.all_to_all(payload, "z", 0, 0, tiled=True)
     blocks = jnp.broadcast_to(blocks[None], (xs, *blocks.shape))
@@ -298,7 +306,7 @@
     blocks = lax.all_to_all(partial.reshape(xs * tps, -1, 2, LANES), ("x", "tp"), 0, 0, tiled=True)
     columns, squares = merge(xs, zs, tps, blocks.reshape(partial.shape))
     got = lax.all_to_all(columns.reshape(zs, 1, -1), "z", 0, 0, tiled=True)
-    return finish(requests, nprobe, cap // tps, route, got.reshape(columns.shape), squares)
+    return finish(requests, nprobe, cap // tps, select, got.reshape(columns.shape), squares)
 
 
 def solution(mesh):

time: 72.5 us -> 71.8 us (level)
  no operation moved by 1% of the time
where the time goes in v6:
time: 71.8 us; the launch traced here: 71.6 us
  blocking collectives  66.9 us (93%)
  Pallas kernels  4.52 us (6%)
    all_to_all x1, blocking collectives, per_device(): blocks = lax.all_to_all(payload, 'z', 0, 0, tiled=True)  27.2 us
    all_to_all x1, blocking collectives, per_device(): lax.all_to_all(partial.reshape(xs * tps, -1, 2, LANES), ('x', 'tp'), 0, 0...  16.2 us
    all_to_all x1, blocking collectives, per_device(): got = lax.all_to_all(columns.reshape(zs, 1, -1), 'z', 0, 0, tiled=True)  13.9 us
    all_to_all x1, blocking collectives, per_device(): rows = lax.all_to_all(blocks, 'x', 0, 0, tiled=True).reshape(-1, LANES)  9.52 us
    pallas_call x1, Pallas kernels, pool(): pl.pallas_call(functools.partial(pool_kernel, local_slots, xs, zs, tps),...  2.37 us

profile of v6, /device:TPU:1, one launch (start us, length us, event | category | flops | bytes accessed | tf_op | source)
XLA Modules:
  0.0 71.6 jit_solution(4142759296811719411)
XLA Ops:
  0.0 0.0 copy-start
  0.0 2.4 %pool.1 = (bf16[16,9,2,128]{3,2,1,0:T(2,128)(2,1)S(1)}, f32[8,128]{1,0:T(8,128)S(1)}, f32[32,256]{1,0:T(8,128)S(1)}) custom-call(s32[1,4]{1,0:T(1,128)} %lens_hbm.1, s32[4,8]{1,0:T(4,128)} %probes_hbm.1, s32[512]{0:T(512)} %slot_hbm.1, s32[512]{0:T(512)} %size_hbm.1, bf16[512,512]{1,0:T(8,128)(2,1)} %hid_hbm.1, bf16[512,512]{1,0:T(8,128)(2,1)} %lat_hbm.1), custom_call_target="tpu_custom_call" | custom-call | tf_op jit(solution)/shard_map/pool/pallas_call | solution.py:231
  2.4 27.2 %all_to_all.20 = bf16[16,9,2,128]{3,2,1,0:T(2,128)(2,1)S(1)} all-to-all(bf16[16,9,2,128]{3,2,1,0:T(2,128)(2,1)S(1)} %get-tuple-element.11), channel_id=1, replica_groups=mesh['x'=4,'z'=16,'tp'=8] {'z'}, dimensions={0} | all-to-all | bytes 147456 | tf_op jit(solution)/shard_map/all_to_all | solution.py:302
  29.6 0.2 broadcast_in_dim.2
  29.8 9.5 %all_to_all.21 = bf16[4,16,9,2,128]{4,3,2,1,0:T(2,128)(2,1)S(1)} all-to-all(bf16[4,16,9,2,128]{4,3,2,1,0:T(2,128)(2,1)S(1)} %broadcast_in_dim.2), channel_id=1, replica_groups=mesh['x'=4,'z'=16,'tp'=8] {'x'}, dimensions={0} | all-to-all | bytes 589824 | tf_op jit(solution)/shard_map/all_to_all | solution.py:304
  39.3 0.0 copy-done
  39.3 1.1 %score.1 = bf16[320,128]{1,0:T(8,128)(2,1)S(1)} custom-call(bf16[1152,128]{1,0:T(8,128)(2,1)S(1)} %bitcast.6, bf16[1024,512]{1,0:T(8,128)(2,1)S(1)} %bitcast.7, f32[8,128]{1,0:T(8,128)S(1)} %get-tuple-element.12.ss_ref), custom_call_target="tpu_custom_call" | custom-call | tf_op jit(solution)/shard_map/score/pallas_call | solution.py:259
  40.4 16.2 %all_to_all.22 = bf16[32,5,2,128]{3,2,1,0:T(2,128)(2,1)S(1)} all-to-all(bf16[32,5,2,128]{3,2,1,0:T(2,128)(2,1)S(1)} %bitcast.8), channel_id=1, replica_groups=mesh['x'=4,'z'=16,'tp'=8] {'x','tp'}, dimensions={0} | all-to-all | bytes 163840 | tf_op jit(solution)/shard_map/all_to_all | solution.py:306
  56.6 0.1 merge.1
  56.7 13.9 %all_to_all.23 = f32[16,1,256]{2,1,0:T(1,128)S(1)} all-to-all(f32[16,1,256]{2,1,0:T(1,128)S(1)} %bitcast.11), channel_id=1, replica_groups=mesh['x'=4,'z'=16,'tp'=8] {'z'}, dimensions={0} | all-to-all | bytes 32768 | tf_op jit(solution)/shard_map/all_to_all | solution.py:308
  70.6 0.9 %finish.1 = f32[4,8,16]{2,1,0:T(8,128)} custom-call(f32[32,256]{1,0:T(8,128)S(1)} %get-tuple-element.10.sel_ref, f32[32,128]{1,0:T(8,128)S(1)} %bitcast.10, f32[8,128]{1,0:T(8,128)S(1)} %get-tuple-element.14.ss_ref), custom_call_target="tpu_custom_call" | custom-call | tf_op jit(solution)/shard_map/finish/pallas_call | solution.py:286
Async XLA Ops:
  0.0 39.3 %copy-start = (bf16[8,128,512]{2,1,0:T(8,128)(2,1)S(1)}, bf16[8,128,512]{2,1,0:T(8,128)(2,1)}, u32[]{:S(2)}) copy-start(bf16[8,128,512]{2,1,0:T(8,128)(2,1)} %param.13) | copy-start | bytes 3145732

commit v7 on v6

--- a/solution.py
+++ b/solution.py
@@ -149,9 +149,12 @@
     chosen = jnp.concatenate(chosen, axis=0).astype(jnp.bfloat16)
     local = code & (local_slots - 1)
     total = jnp.zeros((MOST * owners, cap), jnp.float32)
-    for s in range(local_slots):
-        got = lax.dot_general(chosen, pas_ref[s * cap : (s + 1) * cap, :], NT, preferred_element_type=jnp.float32)
-        total = total + jnp.where(local == s, got, 0.0)
+    for s in range(0, local_slots, 2):
+        got = lax.dot_general(
+            chosen, pas_ref[s * cap : (s + 2) * cap, :], NT, preferred_element_type=jnp.float32
+        )
+        total = jnp.where(local == s, got[:, :cap], total)
+        total = jnp.where(local == s + 1, got[:, cap:], total)
 
     tps = zs // GROUP * MOST
     part = LANES // tps

time: 71.8 us -> 71.6 us (level)
  no operation moved by 1% of the time
where the time goes in v7:
time: 71.6 us; the launch traced here: 71.3 us
  blocking collectives  66.9 us (93%)
  Pallas kernels  4.25 us (6%)
    all_to_all x1, blocking collectives, per_device(): blocks = lax.all_to_all(payload, 'z', 0, 0, tiled=True)  27.2 us
    all_to_all x1, blocking collectives, per_device(): lax.all_to_all(partial.reshape(xs * tps, -1, 2, LANES), ('x', 'tp'), 0, 0...  16.2 us
    all_to_all x1, blocking collectives, per_device(): got = lax.all_to_all(columns.reshape(zs, 1, -1), 'z', 0, 0, tiled=True)  13.9 us
    all_to_all x1, blocking collectives, per_device(): rows = lax.all_to_all(blocks, 'x', 0, 0, tiled=True).reshape(-1, LANES)  9.52 us
    pallas_call x1, Pallas kernels, pool(): pl.pallas_call(functools.partial(pool_kernel, local_slots, xs, zs, tps),...  2.37 us

profile of v7, /device:TPU:1, one launch (start us, length us, event | category | flops | bytes accessed | tf_op | source)
XLA Modules:
  0.0 71.3 jit_solution(2275183019599832684)
XLA Ops:
  0.0 0.0 copy-start
  0.0 2.4 %pool.1 = (bf16[16,9,2,128]{3,2,1,0:T(2,128)(2,1)S(1)}, f32[8,128]{1,0:T(8,128)S(1)}, f32[32,256]{1,0:T(8,128)S(1)}) custom-call(s32[1,4]{1,0:T(1,128)} %lens_hbm.1, s32[4,8]{1,0:T(4,128)} %probes_hbm.1, s32[512]{0:T(512)} %slot_hbm.1, s32[512]{0:T(512)} %size_hbm.1, bf16[512,512]{1,0:T(8,128)(2,1)} %hid_hbm.1, bf16[512,512]{1,0:T(8,128)(2,1)} %lat_hbm.1), custom_call_target="tpu_custom_call" | custom-call | tf_op jit(solution)/shard_map/pool/pallas_call | solution.py:234
  2.4 27.2 %all_to_all.20 = bf16[16,9,2,128]{3,2,1,0:T(2,128)(2,1)S(1)} all-to-all(bf16[16,9,2,128]{3,2,1,0:T(2,128)(2,1)S(1)} %get-tuple-element.11), channel_id=1, replica_groups=mesh['x'=4,'z'=16,'tp'=8] {'z'}, dimensions={0} | all-to-all | bytes 147456 | tf_op jit(solution)/shard_map/all_to_all | solution.py:305
  29.6 0.2 broadcast_in_dim.2
  29.8 9.5 %all_to_all.21 = bf16[4,16,9,2,128]{4,3,2,1,0:T(2,128)(2,1)S(1)} all-to-all(bf16[4,16,9,2,128]{4,3,2,1,0:T(2,128)(2,1)S(1)} %broadcast_in_dim.2), channel_id=1, replica_groups=mesh['x'=4,'z'=16,'tp'=8] {'x'}, dimensions={0} | all-to-all | bytes 589824 | tf_op jit(solution)/shard_map/all_to_all | solution.py:307
  39.3 0.0 copy-done
  39.3 0.8 %score.1 = bf16[320,128]{1,0:T(8,128)(2,1)S(1)} custom-call(bf16[1152,128]{1,0:T(8,128)(2,1)S(1)} %bitcast.6, bf16[1024,512]{1,0:T(8,128)(2,1)S(1)} %bitcast.7, f32[8,128]{1,0:T(8,128)S(1)} %get-tuple-element.12.ss_ref), custom_call_target="tpu_custom_call" | custom-call | tf_op jit(solution)/shard_map/score/pallas_call | solution.py:262
  40.2 16.2 %all_to_all.22 = bf16[32,5,2,128]{3,2,1,0:T(2,128)(2,1)S(1)} all-to-all(bf16[32,5,2,128]{3,2,1,0:T(2,128)(2,1)S(1)} %bitcast.8), channel_id=1, replica_groups=mesh['x'=4,'z'=16,'tp'=8] {'x','tp'}, dimensions={0} | all-to-all | bytes 163840 | tf_op jit(solution)/shard_map/all_to_all | solution.py:309
  56.3 0.1 merge.1
  56.4 13.9 %all_to_all.23 = f32[16,1,256]{2,1,0:T(1,128)S(1)} all-to-all(f32[16,1,256]{2,1,0:T(1,128)S(1)} %bitcast.11), channel_id=1, replica_groups=mesh['x'=4,'z'=16,'tp'=8] {'z'}, dimensions={0} | all-to-all | bytes 32768 | tf_op jit(solution)/shard_map/all_to_all | solution.py:311
  70.4 0.9 %finish.1 = f32[4,8,16]{2,1,0:T(8,128)} custom-call(f32[32,256]{1,0:T(8,128)S(1)} %get-tuple-element.10.sel_ref, f32[32,128]{1,0:T(8,128)S(1)} %bitcast.10, f32[8,128]{1,0:T(8,128)S(1)} %get-tuple-element.14.ss_ref), custom_call_target="tpu_custom_call" | custom-call | tf_op jit(solution)/shard_map/finish/pallas_call | solution.py:289
Async XLA Ops:
  0.0 39.3 %copy-start = (bf16[8,128,512]{2,1,0:T(8,128)(2,1)S(1)}, bf16[8,128,512]{2,1,0:T(8,128)(2,1)}, u32[]{:S(2)}) copy-start(bf16[8,128,512]{2,1,0:T(8,128)(2,1)} %param.13) | copy-start | bytes 3145732

commit v8 on v7

--- a/solution.py
+++ b/solution.py
@@ -127,7 +127,7 @@
     block = rows_ref.shape[0] // owners
     bits = local_slots.bit_length() - 1
     me = (lax.axis_index(("x", "z")) * MOST).astype(jnp.float32)
-    rows[...] = rows_ref[...].astype(jnp.float32)
+    rows[: rows_ref.shape[0], :] = rows_ref[...].astype(jnp.float32)
     place = rows[pl.ds(requests * pieces, owners, stride=block), :]
     code = rows[pl.ds(requests * pieces + 1, owners, stride=block), :]
     mine = jnp.concatenate([jnp.where(place == me + float(k), code, 0.0) for k in range(MOST)], axis=0)
@@ -182,9 +182,9 @@
     out_ref[...] = blocks[...].astype(jnp.bfloat16)
 
 
-def merge_kernel(xs, tps, got_ref, out_ref, ss_ref, blocks):
-    height = blocks.shape[0] // (xs * tps)
-    blocks[...] = got_ref[...].astype(jnp.float32)
+def merge_kernel(xs, tps, got_ref, out_ref, ss_ref, blocks, columns):
+    height = got_ref.shape[0] // (xs * tps)
+    blocks[: got_ref.shape[0], :] = got_ref[...].astype(jnp.float32)
     total = []
     for x in range(xs):
         acc = blocks[x * tps * height : x * tps * height + GROUP, :]
@@ -198,8 +198,9 @@
         one, two = total[2 * r], total[2 * r + 1]
         near = jnp.where(left, one, pltpu.roll(two, LANES // 2, 1))
         far = jnp.where(left, pltpu.roll(one, LANES // 2, 1), two)
-        out_ref[pl.ds(r, GROUP, stride=halves), :] = near
-        out_ref[pl.ds(GROUP * halves + r, GROUP, stride=halves), :] = far
+        columns[pl.ds(r, GROUP, stride=halves), :] = near
+        columns[pl.ds(GROUP * halves + r, GROUP, stride=halves), :] = far
+    out_ref[...] = columns[: out_ref.shape[0], :]
     mine = lax.axis_index("x") * (tps * height) + GROUP
     top = blocks[pl.ds(mine, 1), :]
     low = blocks[pl.ds(mine + 1, 1), :]
@@ -264,7 +265,10 @@
         out_shape=jax.ShapeDtypeStruct(blocks, jnp.bfloat16),
         in_specs=[VMEM, VMEM, VMEM],
         out_specs=VMEM,
-        scratch_shapes=[pltpu.VMEM(rows.shape, jnp.float32), pltpu.VMEM(blocks, jnp.float32)],
+        scratch_shapes=[
+            pltpu.VMEM((rows.shape[0] + 3 * GROUP, LANES), jnp.float32),
+            pltpu.VMEM(blocks, jnp.float32),
+        ],
         name="score",
         compiler_params=PARAMS,
     )(rows, passages.reshape(local_slots * cap, width), squares)
@@ -279,7 +283,10 @@
         ),
         in_specs=[VMEM],
         out_specs=(VMEM, VMEM),
-        scratch_shapes=[pltpu.VMEM(got.shape, jnp.float32)],
+        scratch_shapes=[
+            pltpu.VMEM((got.shape[0] + GROUP, LANES), jnp.float32),
+            pltpu.VMEM((zs * xs // 2 + GROUP, LANES), jnp.float32),
+        ],
         name="merge",
         compiler_params=PARAMS,
     )(got)

time: 71.6 us -> 71.5 us (level)
  no operation moved by 1% of the time
where the time goes in v8:
time: 71.5 us; the launch traced here: 71.3 us
  blocking collectives  66.9 us (94%)
  Pallas kernels  4.24 us (6%)
    all_to_all x1, blocking collectives, per_device(): blocks = lax.all_to_all(payload, 'z', 0, 0, tiled=True)  27.2 us
    all_to_all x1, blocking collectives, per_device(): lax.all_to_all(partial.reshape(xs * tps, -1, 2, LANES), ('x', 'tp'), 0, 0...  16.2 us
    all_to_all x1, blocking collectives, per_device(): got = lax.all_to_all(columns.reshape(zs, 1, -1), 'z', 0, 0, tiled=True)  13.9 us
    all_to_all x1, blocking collectives, per_device(): rows = lax.all_to_all(blocks, 'x', 0, 0, tiled=True).reshape(-1, LANES)  9.52 us
    pallas_call x1, Pallas kernels, pool(): pl.pallas_call(functools.partial(pool_kernel, local_slots, xs, zs, tps),...  2.37 us

profile of v8, /device:TPU:1, one launch (start us, length us, event | category | flops | bytes accessed | tf_op | source)
XLA Modules:
  0.0 71.3 jit_solution(11544499901091796000)
XLA Ops:
  0.0 0.0 copy-start
  0.0 2.4 %pool.1 = (bf16[16,9,2,128]{3,2,1,0:T(2,128)(2,1)S(1)}, f32[8,128]{1,0:T(8,128)S(1)}, f32[32,256]{1,0:T(8,128)S(1)}) custom-call(s32[1,4]{1,0:T(1,128)} %lens_hbm.1, s32[4,8]{1,0:T(4,128)} %probes_hbm.1, s32[512]{0:T(512)} %slot_hbm.1, s32[512]{0:T(512)} %size_hbm.1, bf16[512,512]{1,0:T(8,128)(2,1)} %hid_hbm.1, bf16[512,512]{1,0:T(8,128)(2,1)} %lat_hbm.1), custom_call_target="tpu_custom_call" | custom-call | tf_op jit(solution)/shard_map/pool/pallas_call | solution.py:235
  2.4 27.2 %all_to_all.20 = bf16[16,9,2,128]{3,2,1,0:T(2,128)(2,1)S(1)} all-to-all(bf16[16,9,2,128]{3,2,1,0:T(2,128)(2,1)S(1)} %get-tuple-element.11), channel_id=1, replica_groups=mesh['x'=4,'z'=16,'tp'=8] {'z'}, dimensions={0} | all-to-all | bytes 147456 | tf_op jit(solution)/shard_map/all_to_all | solution.py:312
  29.6 0.2 broadcast_in_dim.2
  29.8 9.5 %all_to_all.21 = bf16[4,16,9,2,128]{4,3,2,1,0:T(2,128)(2,1)S(1)} all-to-all(bf16[4,16,9,2,128]{4,3,2,1,0:T(2,128)(2,1)S(1)} %broadcast_in_dim.2), channel_id=1, replica_groups=mesh['x'=4,'z'=16,'tp'=8] {'x'}, dimensions={0} | all-to-all | bytes 589824 | tf_op jit(solution)/shard_map/all_to_all | solution.py:314
  39.3 0.0 copy-done
  39.3 0.8 %score.1 = bf16[320,128]{1,0:T(8,128)(2,1)S(1)} custom-call(bf16[1152,128]{1,0:T(8,128)(2,1)S(1)} %bitcast.6, bf16[1024,512]{1,0:T(8,128)(2,1)S(1)} %bitcast.7, f32[8,128]{1,0:T(8,128)S(1)} %get-tuple-element.12.ss_ref), custom_call_target="tpu_custom_call" | custom-call | tf_op jit(solution)/shard_map/score/pallas_call | solution.py:263
  40.1 16.2 %all_to_all.22 = bf16[32,5,2,128]{3,2,1,0:T(2,128)(2,1)S(1)} all-to-all(bf16[32,5,2,128]{3,2,1,0:T(2,128)(2,1)S(1)} %bitcast.8), channel_id=1, replica_groups=mesh['x'=4,'z'=16,'tp'=8] {'x','tp'}, dimensions={0} | all-to-all | bytes 163840 | tf_op jit(solution)/shard_map/all_to_all | solution.py:316
  56.3 0.1 merge.1
  56.4 13.9 %all_to_all.23 = f32[16,1,256]{2,1,0:T(1,128)S(1)} all-to-all(f32[16,1,256]{2,1,0:T(1,128)S(1)} %bitcast.11), channel_id=1, replica_groups=mesh['x'=4,'z'=16,'tp'=8] {'z'}, dimensions={0} | all-to-all | bytes 32768 | tf_op jit(solution)/shard_map/all_to_all | solution.py:318
  70.3 0.9 %finish.1 = f32[4,8,16]{2,1,0:T(8,128)} custom-call(f32[32,256]{1,0:T(8,128)S(1)} %get-tuple-element.10.sel_ref, f32[32,128]{1,0:T(8,128)S(1)} %bitcast.10, f32[8,128]{1,0:T(8,128)S(1)} %get-tuple-element.14.ss_ref), custom_call_target="tpu_custom_call" | custom-call | tf_op jit(solution)/shard_map/finish/pallas_call | solution.py:296
Async XLA Ops:
  0.0 39.3 %copy-start = (bf16[8,128,512]{2,1,0:T(8,128)(2,1)S(1)}, bf16[8,128,512]{2,1,0:T(8,128)(2,1)}, u32[]{:S(2)}) copy-start(bf16[8,128,512]{2,1,0:T(8,128)(2,1)} %param.13) | copy-start | bytes 3145732

commit v9 on v8

--- a/solution.py
+++ b/solution.py
@@ -13,6 +13,7 @@
 LANES = 128
 GROUP = 8
 XS = 4
+PACK_ROWS = 18
 VMEM = pl.BlockSpec(memory_space=pltpu.VMEM)
 HBM = pl.BlockSpec(memory_space=pltpu.HBM)
 NT = (((1,), (1,)), ((), ()))
@@ -60,8 +61,8 @@
     part = LANES // tps
     column = (spot & (part - 1)) + lax.axis_index("tp") * part
     group_of = lax.shift_right_logical(spot, part.bit_length() - 1)
+    items = requests * nprobe
     lane = lax.broadcasted_iota(jnp.int32, (2, LANES), 1)
-    first = lax.broadcasted_iota(jnp.int32, (2, LANES), 0) == 0
     marks = jnp.full((2, LANES), -1, jnp.int32)
     for query in range(requests):
         for j in range(nprobe):
@@ -78,7 +79,7 @@
             sel_ref[item : item + 1, :LANES] = jnp.where(spot == row, 1.0, 0.0)
             sel_ref[item : item + 1, LANES:] = jnp.where(here, 1.0, 0.0)
             code = (query << bits) + (slot & (local_slots - 1))
-            marks = jnp.where(lane == item, jnp.where(first, place, code), marks)
+            marks = jnp.where(lane == item, place, jnp.where(lane == items + item, code, marks))
     marks = marks.astype(jnp.float32).astype(jnp.bfloat16)
     for copy in copies[4:]:
         copy.wait()
@@ -120,22 +121,35 @@
         pay_ref[place, requests * pairs] = marks
 
 
-def score_kernel(local_slots, xs, zs, requests, rows_ref, pas_ref, ss_ref, out_ref, rows, blocks):
+def spread_kernel(got_ref, out_ref, rows):
+    copies = out_ref.shape[0]
+    packs = got_ref.shape[0] // PACK_ROWS
+    rows[: got_ref.shape[0], :] = got_ref[...].astype(jnp.float32)
+    pieces = [rows[pl.ds(i, packs, stride=PACK_ROWS), :] for i in range(PACK_ROWS - 1)]
+    block = jnp.concatenate(pieces, axis=0).astype(jnp.bfloat16)
+    for x in range(copies):
+        out_ref[x] = block
+
+
+def score_kernel(local_slots, xs, zs, requests, items, rows_ref, pas_ref, ss_ref, out_ref, blocks):
     owners = xs * zs
     cap = LANES
     pieces = pas_ref.shape[1] // LANES
-    block = rows_ref.shape[0] // owners
     bits = local_slots.bit_length() - 1
     me = (lax.axis_index(("x", "z")) * MOST).astype(jnp.float32)
-    rows[: rows_ref.shape[0], :] = rows_ref[...].astype(jnp.float32)
-    place = rows[pl.ds(requests * pieces, owners, stride=block), :]
-    code = rows[pl.ds(requests * pieces + 1, owners, stride=block), :]
+
+    def piece_of(i):
+        starts = [x * (rows_ref.shape[0] // xs) + i * zs for x in range(xs)]
+        return jnp.concatenate([rows_ref[r : r + zs, :] for r in starts], axis=0).astype(jnp.float32)
+
+    marks = piece_of(requests * pieces)
+    lane = lax.broadcasted_iota(jnp.int32, marks.shape, 1)
+    place = jnp.where(lane < items, marks, -1.0)
+    code = pltpu.roll(marks, LANES - items, 1)
     mine = jnp.concatenate([jnp.where(place == me + float(k), code, 0.0) for k in range(MOST)], axis=0)
     ones = jnp.ones((LANES, LANES), jnp.bfloat16)
     code = jnp.dot(mine.astype(jnp.bfloat16), ones, preferred_element_type=jnp.float32).astype(jnp.int32)
-    pieces_of = [
-        [rows[pl.ds(q * pieces + f, owners, stride=block), :] for f in range(pieces)] for q in range(requests)
-    ]
+    pieces_of = [[piece_of(q * pieces + f) for f in range(pieces)] for q in range(requests)]
     chosen = []
     for k in range(MOST):
         query = lax.shift_right_logical(code[k * owners : (k + 1) * owners], bits)
@@ -257,16 +271,27 @@
     )(*(pltpu.with_memory_space_constraint(x, pltpu.HBM) for x in operands))
 
 
-def score(xs, zs, tps, requests, rows, passages, squares):
+def spread(xs, zs, got):
+    return pl.pallas_call(
+        spread_kernel,
+        out_shape=jax.ShapeDtypeStruct((xs, zs * (PACK_ROWS - 1), LANES), jnp.bfloat16),
+        in_specs=[VMEM],
+        out_specs=VMEM,
+        scratch_shapes=[pltpu.VMEM((got.shape[0] + 3 * GROUP, LANES), jnp.float32)],
+        name="spread",
+        compiler_params=PARAMS,
+    )(got)
+
+
+def score(xs, zs, tps, requests, items, rows, passages, squares):
     local_slots, cap, width = passages.shape
     blocks = (xs * tps * (GROUP + 2), LANES)
     return pl.pallas_call(
-        functools.partial(score_kernel, local_slots, xs, zs, requests),
+        functools.partial(score_kernel, local_slots, xs, zs, requests, items),
         out_shape=jax.ShapeDtypeStruct(blocks, jnp.bfloat16),
         in_specs=[VMEM, VMEM, VMEM],
         out_specs=VMEM,
         scratch_shapes=[
-            pltpu.VMEM((rows.shape[0] + 3 * GROUP, LANES), jnp.float32),
             pltpu.VMEM(blocks, jnp.float32),
         ],
         name="score",
@@ -310,9 +335,9 @@
         local_slots, xs, zs, tps, lengths, probes, cluster_slot, slab_sizes, hidden, latents
     )
     blocks = lax.all_to_all(payload, "z", 0, 0, tiled=True)
-    blocks = jnp.broadcast_to(blocks[None], (xs, *blocks.shape))
+    blocks = spread(xs, zs, blocks.reshape(-1, LANES))
     rows = lax.all_to_all(blocks, "x", 0, 0, tiled=True).reshape(-1, LANES)
-    partial = score(xs, zs, tps, requests, rows, passages, squares)
+    partial = score(xs, zs, tps, requests, requests * nprobe, rows, passages, squares)
     blocks = lax.all_to_all(partial.reshape(xs * tps, -1, 2, LANES), ("x", "tp"), 0, 0, tiled=True)
     columns, squares = merge(xs, zs, tps, blocks.reshape(partial.shape))
     got = lax.all_to_all(columns.reshape(zs, 1, -1), "z", 0, 0, tiled=True)

time: 71.5 us -> 71.4 us (level)
  no operation moved by 1% of the time
where the time goes in v9:
time: 71.4 us; the launch traced here: 71.1 us
  blocking collectives  66.8 us (94%)
  Pallas kernels  4.3 us (6%)
    all_to_all x1, blocking collectives, per_device(): blocks = lax.all_to_all(payload, 'z', 0, 0, tiled=True)  27.2 us
    all_to_all x1, blocking collectives, per_device(): lax.all_to_all(partial.reshape(xs * tps, -1, 2, LANES), ('x', 'tp'), 0, 0...  16.2 us
    all_to_all x1, blocking collectives, per_device(): got = lax.all_to_all(columns.reshape(zs, 1, -1), 'z', 0, 0, tiled=True)  13.9 us
    all_to_all x1, blocking collectives, per_device(): rows = lax.all_to_all(blocks, 'x', 0, 0, tiled=True).reshape(-1, LANES)  9.43 us
    pallas_call x1, Pallas kernels, pool(): pl.pallas_call(functools.partial(pool_kernel, local_slots, xs, zs, tps),...  2.37 us

profile of v9, /device:TPU:1, one launch (start us, length us, event | category | flops | bytes accessed | tf_op | source)
XLA Modules:
  0.0 71.1 jit_solution(11462493113414622998)
XLA Ops:
  0.0 0.0 copy-start
  0.0 2.4 %pool.1 = (bf16[16,9,2,128]{3,2,1,0:T(2,128)(2,1)S(1)}, f32[8,128]{1,0:T(8,128)S(1)}, f32[32,256]{1,0:T(8,128)S(1)}) custom-call(s32[1,4]{1,0:T(1,128)} %lens_hbm.1, s32[4,8]{1,0:T(4,128)} %probes_hbm.1, s32[512]{0:T(512)} %slot_hbm.1, s32[512]{0:T(512)} %size_hbm.1, bf16[512,512]{1,0:T(8,128)(2,1)} %hid_hbm.1, bf16[512,512]{1,0:T(8,128)(2,1)} %lat_hbm.1), custom_call_target="tpu_custom_call" | custom-call | tf_op jit(solution)/shard_map/pool/pallas_call | solution.py:249
  2.4 27.2 %all_to_all.20 = bf16[16,9,2,128]{3,2,1,0:T(2,128)(2,1)S(1)} all-to-all(bf16[16,9,2,128]{3,2,1,0:T(2,128)(2,1)S(1)} %get-tuple-element.11), channel_id=1, replica_groups=mesh['x'=4,'z'=16,'tp'=8] {'z'}, dimensions={0} | all-to-all | bytes 147456 | tf_op jit(solution)/shard_map/all_to_all | solution.py:337
  29.7 9.4 %all_to_all.21 = bf16[4,272,128]{2,1,0:T(8,128)(2,1)S(1)} all-to-all(bf16[4,272,128]{2,1,0:T(8,128)(2,1)S(1)} %spread.1), channel_id=1, replica_groups=mesh['x'=4,'z'=16,'tp'=8] {'x'}, dimensions={0} | all-to-all | bytes 557056 | tf_op jit(solution)/shard_map/all_to_all | solution.py:339
  39.1 0.0 copy-done
  39.1 0.8 %score.1 = bf16[320,128]{1,0:T(8,128)(2,1)S(1)} custom-call(bf16[1088,128]{1,0:T(8,128)(2,1)S(1)} %bitcast.7, bf16[1024,512]{1,0:T(8,128)(2,1)S(1)} %bitcast.8, f32[8,128]{1,0:T(8,128)S(1)} %get-tuple-element.12.ss_ref), custom_call_target="tpu_custom_call" | custom-call | tf_op jit(solution)/shard_map/score/pallas_call | solution.py:289
  40.0 16.2 %all_to_all.22 = bf16[32,5,2,128]{3,2,1,0:T(2,128)(2,1)S(1)} all-to-all(bf16[32,5,2,128]{3,2,1,0:T(2,128)(2,1)S(1)} %bitcast.9), channel_id=1, replica_groups=mesh['x'=4,'z'=16,'tp'=8] {'x','tp'}, dimensions={0} | all-to-all | bytes 163840 | tf_op jit(solution)/shard_map/all_to_all | solution.py:341
  56.1 0.1 merge.1
  56.2 13.9 %all_to_all.23 = f32[16,1,256]{2,1,0:T(1,128)S(1)} all-to-all(f32[16,1,256]{2,1,0:T(1,128)S(1)} %bitcast.13), channel_id=1, replica_groups=mesh['x'=4,'z'=16,'tp'=8] {'z'}, dimensions={0} | all-to-all | bytes 32768 | tf_op jit(solution)/shard_map/all_to_all | solution.py:343
  70.2 0.9 %finish.1 = f32[4,8,16]{2,1,0:T(8,128)} custom-call(f32[32,256]{1,0:T(8,128)S(1)} %get-tuple-element.10.sel_ref, f32[32,128]{1,0:T(8,128)S(1)} %bitcast.12, f32[8,128]{1,0:T(8,128)S(1)} %get-tuple-element.14.ss_ref), custom_call_target="tpu_custom_call" | custom-call | tf_op jit(solution)/shard_map/finish/pallas_call | solution.py:321
  (1 shorter events, 0.0 us)
Async XLA Ops:
  0.0 39.1 %copy-start = (bf16[8,128,512]{2,1,0:T(8,128)(2,1)S(1)}, bf16[8,128,512]{2,1,0:T(8,128)(2,1)}, u32[]{:S(2)}) copy-start(bf16[8,128,512]{2,1,0:T(8,128)(2,1)} %param.13) | copy-start | bytes 3145732

commit v10 on v9

--- a/solution.py
+++ b/solution.py
@@ -147,8 +147,7 @@
     place = jnp.where(lane < items, marks, -1.0)
     code = pltpu.roll(marks, LANES - items, 1)
     mine = jnp.concatenate([jnp.where(place == me + float(k), code, 0.0) for k in range(MOST)], axis=0)
-    ones = jnp.ones((LANES, LANES), jnp.bfloat16)
-    code = jnp.dot(mine.astype(jnp.bfloat16), ones, preferred_element_type=jnp.float32).astype(jnp.int32)
+    code = jnp.broadcast_to(jnp.sum(mine, axis=1, keepdims=True), mine.shape).astype(jnp.int32)
     pieces_of = [[piece_of(q * pieces + f) for f in range(pieces)] for q in range(requests)]
     chosen = []
     for k in range(MOST):
@@ -182,7 +181,6 @@
             mixed = skew[0]
             for g in range(1, tps):
                 mixed = jnp.where(lane // part == (t + g) % tps, skew[g], mixed)
-            mixed = pltpu.roll(mixed, LANES - part * t, 1) if t else mixed
             row = (x * tps + t) * height
             blocks[row : row + GROUP, :] = mixed
     lane = lax.broadcasted_iota(jnp.int32, (1, LANES), 1)
@@ -205,7 +203,8 @@
         for t in range(1, tps):
             row = (x * tps + t) * height
             acc = acc + blocks[row : row + GROUP, :]
-        total.append(acc)
+        turn = LANES - lax.axis_index("tp") * (LANES // tps)
+        total.append(pltpu.roll(acc, turn, 1))
     left = lax.broadcasted_iota(jnp.int32, (GROUP, LANES), 1) < LANES // 2
     halves = xs // 2
     for r in range(halves):

time: 71.4 us -> 71.3 us (level)
  no operation moved by 1% of the time
where the time goes in v10:
time: 71.3 us; the launch traced here: 71 us
  blocking collectives  66.8 us (94%)
  Pallas kernels  4.22 us (6%)
    all_to_all x1, blocking collectives, per_device(): blocks = lax.all_to_all(payload, 'z', 0, 0, tiled=True)  27.2 us
    all_to_all x1, blocking collectives, per_device(): lax.all_to_all(partial.reshape(xs * tps, -1, 2, LANES), ('x', 'tp'), 0, 0...  16.2 us
    all_to_all x1, blocking collectives, per_device(): got = lax.all_to_all(columns.reshape(zs, 1, -1), 'z', 0, 0, tiled=True)  13.9 us
    all_to_all x1, blocking collectives, per_device(): rows = lax.all_to_all(blocks, 'x', 0, 0, tiled=True).reshape(-1, LANES)  9.43 us
    pallas_call x1, Pallas kernels, pool(): pl.pallas_call(functools.partial(pool_kernel, local_slots, xs, zs, tps),...  2.37 us

profile of v10, /device:TPU:1, one launch (start us, length us, event | category | flops | bytes accessed | tf_op | source)
XLA Modules:
  0.0 71.0 jit_solution(11032882873335293733)
XLA Ops:
  0.0 0.0 copy-start
  0.0 2.4 %pool.1 = (bf16[16,9,2,128]{3,2,1,0:T(2,128)(2,1)S(1)}, f32[8,128]{1,0:T(8,128)S(1)}, f32[32,256]{1,0:T(8,128)S(1)}) custom-call(s32[1,4]{1,0:T(1,128)} %lens_hbm.1, s32[4,8]{1,0:T(4,128)} %probes_hbm.1, s32[512]{0:T(512)} %slot_hbm.1, s32[512]{0:T(512)} %size_hbm.1, bf16[512,512]{1,0:T(8,128)(2,1)} %hid_hbm.1, bf16[512,512]{1,0:T(8,128)(2,1)} %lat_hbm.1), custom_call_target="tpu_custom_call" | custom-call | tf_op jit(solution)/shard_map/pool/pallas_call | solution.py:248
  2.4 27.2 %all_to_all.20 = bf16[16,9,2,128]{3,2,1,0:T(2,128)(2,1)S(1)} all-to-all(bf16[16,9,2,128]{3,2,1,0:T(2,128)(2,1)S(1)} %get-tuple-element.11), channel_id=1, replica_groups=mesh['x'=4,'z'=16,'tp'=8] {'z'}, dimensions={0} | all-to-all | bytes 147456 | tf_op jit(solution)/shard_map/all_to_all | solution.py:336
  29.7 9.4 %all_to_all.21 = bf16[4,272,128]{2,1,0:T(8,128)(2,1)S(1)} all-to-all(bf16[4,272,128]{2,1,0:T(8,128)(2,1)S(1)} %spread.1), channel_id=1, replica_groups=mesh['x'=4,'z'=16,'tp'=8] {'x'}, dimensions={0} | all-to-all | bytes 557056 | tf_op jit(solution)/shard_map/all_to_all | solution.py:338
  39.1 0.0 copy-done
  39.1 0.7 score.1
  39.8 16.2 %all_to_all.22 = bf16[32,5,2,128]{3,2,1,0:T(2,128)(2,1)S(1)} all-to-all(bf16[32,5,2,128]{3,2,1,0:T(2,128)(2,1)S(1)} %bitcast.9), channel_id=1, replica_groups=mesh['x'=4,'z'=16,'tp'=8] {'x','tp'}, dimensions={0} | all-to-all | bytes 163840 | tf_op jit(solution)/shard_map/all_to_all | solution.py:340
  56.0 0.2 merge.1
  56.2 13.9 %all_to_all.23 = f32[16,1,256]{2,1,0:T(1,128)S(1)} all-to-all(f32[16,1,256]{2,1,0:T(1,128)S(1)} %bitcast.13), channel_id=1, replica_groups=mesh['x'=4,'z'=16,'tp'=8] {'z'}, dimensions={0} | all-to-all | bytes 32768 | tf_op jit(solution)/shard_map/all_to_all | solution.py:342
  70.1 0.9 %finish.1 = f32[4,8,16]{2,1,0:T(8,128)} custom-call(f32[32,256]{1,0:T(8,128)S(1)} %get-tuple-element.10.sel_ref, f32[32,128]{1,0:T(8,128)S(1)} %bitcast.12, f32[8,128]{1,0:T(8,128)S(1)} %get-tuple-element.14.ss_ref), custom_call_target="tpu_custom_call" | custom-call | tf_op jit(solution)/shard_map/finish/pallas_call | solution.py:320
  (1 shorter events, 0.0 us)
Async XLA Ops:
  0.0 39.1 %copy-start = (bf16[8,128,512]{2,1,0:T(8,128)(2,1)S(1)}, bf16[8,128,512]{2,1,0:T(8,128)(2,1)}, u32[]{:S(2)}) copy-start(bf16[8,128,512]{2,1,0:T(8,128)(2,1)} %param.13) | copy-start | bytes 3145732

commit v11 on v10

--- a/solution.py
+++ b/solution.py
@@ -140,9 +140,9 @@
 
     def piece_of(i):
         starts = [x * (rows_ref.shape[0] // xs) + i * zs for x in range(xs)]
-        return jnp.concatenate([rows_ref[r : r + zs, :] for r in starts], axis=0).astype(jnp.float32)
-
-    marks = piece_of(requests * pieces)
+        return jnp.concatenate([rows_ref[r : r + zs, :] for r in starts], axis=0)
+
+    marks = piece_of(requests * pieces).astype(jnp.float32)
     lane = lax.broadcasted_iota(jnp.int32, marks.shape, 1)
     place = jnp.where(lane < items, marks, -1.0)
     code = pltpu.roll(marks, LANES - items, 1)
@@ -152,14 +152,15 @@
     chosen = []
     for k in range(MOST):
         query = lax.shift_right_logical(code[k * owners : (k + 1) * owners], bits)
+        query = query.astype(jnp.float32).astype(jnp.bfloat16)
         piece = []
         for f in range(pieces):
             got = pieces_of[0][f]
             for q in range(1, requests):
-                got = jnp.where(query == q, pieces_of[q][f], got)
+                got = jnp.where(query == jnp.bfloat16(q), pieces_of[q][f], got)
             piece.append(got)
         chosen.append(jnp.concatenate(piece, axis=1))
-    chosen = jnp.concatenate(chosen, axis=0).astype(jnp.bfloat16)
+    chosen = jnp.concatenate(chosen, axis=0)
     local = code & (local_slots - 1)
     total = jnp.zeros((MOST * owners, cap), jnp.float32)
     for s in range(0, local_slots, 2):

time: 71.3 us -> 71.2 us (level)
  no operation moved by 1% of the time
where the time goes in v11:
time: 71.2 us; the launch traced here: 71 us
  blocking collectives  66.8 us (94%)
  Pallas kernels  4.18 us (6%)
    all_to_all x1, blocking collectives, per_device(): blocks = lax.all_to_all(payload, 'z', 0, 0, tiled=True)  27.2 us
    all_to_all x1, blocking collectives, per_device(): lax.all_to_all(partial.reshape(xs * tps, -1, 2, LANES), ('x', 'tp'), 0, 0...  16.2 us
    all_to_all x1, blocking collectives, per_device(): got = lax.all_to_all(columns.reshape(zs, 1, -1), 'z', 0, 0, tiled=True)  13.9 us
    all_to_all x1, blocking collectives, per_device(): rows = lax.all_to_all(blocks, 'x', 0, 0, tiled=True).reshape(-1, LANES)  9.43 us
    pallas_call x1, Pallas kernels, pool(): pl.pallas_call(functools.partial(pool_kernel, local_slots, xs, zs, tps),...  2.37 us

profile of v11, /device:TPU:1, one launch (start us, length us, event | category | flops | bytes accessed | tf_op | source)
XLA Modules:
  0.0 71.0 jit_solution(3764389686271331830)
XLA Ops:
  0.0 0.0 copy-start
  0.0 2.4 %pool.1 = (bf16[16,9,2,128]{3,2,1,0:T(2,128)(2,1)S(1)}, f32[8,128]{1,0:T(8,128)S(1)}, f32[32,256]{1,0:T(8,128)S(1)}) custom-call(s32[1,4]{1,0:T(1,128)} %lens_hbm.1, s32[4,8]{1,0:T(4,128)} %probes_hbm.1, s32[512]{0:T(512)} %slot_hbm.1, s32[512]{0:T(512)} %size_hbm.1, bf16[512,512]{1,0:T(8,128)(2,1)} %hid_hbm.1, bf16[512,512]{1,0:T(8,128)(2,1)} %lat_hbm.1), custom_call_target="tpu_custom_call" | custom-call | tf_op jit(solution)/shard_map/pool/pallas_call | solution.py:249
  2.4 27.2 %all_to_all.20 = bf16[16,9,2,128]{3,2,1,0:T(2,128)(2,1)S(1)} all-to-all(bf16[16,9,2,128]{3,2,1,0:T(2,128)(2,1)S(1)} %get-tuple-element.11), channel_id=1, replica_groups=mesh['x'=4,'z'=16,'tp'=8] {'z'}, dimensions={0} | all-to-all | bytes 147456 | tf_op jit(solution)/shard_map/all_to_all | solution.py:337
  29.7 9.4 %all_to_all.21 = bf16[4,272,128]{2,1,0:T(8,128)(2,1)S(1)} all-to-all(bf16[4,272,128]{2,1,0:T(8,128)(2,1)S(1)} %spread.1), channel_id=1, replica_groups=mesh['x'=4,'z'=16,'tp'=8] {'x'}, dimensions={0} | all-to-all | bytes 557056 | tf_op jit(solution)/shard_map/all_to_all | solution.py:339
  39.1 0.0 copy-done
  39.1 0.7 score.1
  39.8 16.2 %all_to_all.22 = bf16[32,5,2,128]{3,2,1,0:T(2,128)(2,1)S(1)} all-to-all(bf16[32,5,2,128]{3,2,1,0:T(2,128)(2,1)S(1)} %bitcast.9), channel_id=1, replica_groups=mesh['x'=4,'z'=16,'tp'=8] {'x','tp'}, dimensions={0} | all-to-all | bytes 163840 | tf_op jit(solution)/shard_map/all_to_all | solution.py:341
  56.0 0.2 merge.1
  56.1 13.9 %all_to_all.23 = f32[16,1,256]{2,1,0:T(1,128)S(1)} all-to-all(f32[16,1,256]{2,1,0:T(1,128)S(1)} %bitcast.13), channel_id=1, replica_groups=mesh['x'=4,'z'=16,'tp'=8] {'z'}, dimensions={0} | all-to-all | bytes 32768 | tf_op jit(solution)/shard_map/all_to_all | solution.py:343
  70.0 0.9 %finish.1 = f32[4,8,16]{2,1,0:T(8,128)} custom-call(f32[32,256]{1,0:T(8,128)S(1)} %get-tuple-element.10.sel_ref, f32[32,128]{1,0:T(8,128)S(1)} %bitcast.12, f32[8,128]{1,0:T(8,128)S(1)} %get-tuple-element.14.ss_ref), custom_call_target="tpu_custom_call" | custom-call | tf_op jit(solution)/shard_map/finish/pallas_call | solution.py:321
  (1 shorter events, 0.0 us)
Async XLA Ops:
  0.0 39.1 %copy-start = (bf16[8,128,512]{2,1,0:T(8,128)(2,1)S(1)}, bf16[8,128,512]{2,1,0:T(8,128)(2,1)}, u32[]{:S(2)}) copy-start(bf16[8,128,512]{2,1,0:T(8,128)(2,1)} %param.13) | copy-start | bytes 3145732
